TPU v7x, 256 devices: a whole 4x4x8 slice. The times are simulated.
256 devices in a mesh: wide: 64 (over y_lo, z, x), narrow: 4 (over y_hi, core).
Axes of the slice: x: 4, y: 4 (y_hi: 2, y_lo: 2; y = y_hi * 2 + y_lo), z: 8, core: 2. Of those that a mesh axis runs over, the one named last changes fastest.
Arguments:
- echoes: bfloat16 [2, 4096, 16384], P(None, ('wide', 'narrow')), may hold values from -6 to 6
- chirp_spectrum: float32 [2, 16384], replicated, may hold values from -4 to 4
- fm_rate: float32 [16384], replicated, may hold values from 3.5762787e-05 to 0.00014305115
- range_scale: int32 [16384], replicated, may hold values from -103 to 103
- doppler_curve: int32 [4096], replicated, may hold values from 0 to 4096
- kernels: float32 [8, 8], replicated, may hold values from -2 to 2
Outputs:
- image: bfloat16 [2, 16384, 4096], P(None, ('wide', 'narrow'))
All inputs are finite; a program needn't handle non-finite values.
Results may differ from a plain program's by a relative error of at most 0.034.
Values may be sent and summed in bfloat16 or wider, within the bound.
A program may use at most 128 MiB of HBM per device.

v0:
```python
import math

import jax
import jax.numpy as jnp
from jax import lax
from jax.sharding import PartitionSpec as P

PULSES = 4096
BINS = 16384
INNER = 128
TAPS = 8
PHASES = 8
HALO = 16


def padded_2(cells, sides, width):
    for axis, dim in sides:
        count = lax.axis_size(axis)
        ends = count - 1
        head = lax.slice_in_dim(cells, 0, width, axis=dim)
        tail = lax.slice_in_dim(cells, cells.shape[dim] - width, cells.shape[dim], axis=dim)
        cells = jnp.concatenate(
            [
                lax.ppermute(tail, axis, [(i, (i + 1) % count) for i in range(ends)]),
                cells,
                lax.ppermute(head, axis, [((i + 1) % count, i) for i in range(ends)]),
            ],
            axis=dim,
        )
    return cells


def dft_table(length, exponent_sign, factor):
    counter = jnp.arange(length, dtype=jnp.int32)
    product = counter[:, None] * counter[None, :] % length
    angles = exponent_sign * 2.0 * math.pi / length * product.astype(jnp.float32)
    cosines = jnp.cos(angles) * factor
    sines = jnp.sin(angles) * factor
    upper_rows = jnp.stack([cosines, sines], axis=1)
    lower_rows = jnp.stack([-sines, cosines], axis=1)
    return jnp.stack([upper_rows, lower_rows], axis=0).astype(jnp.bfloat16)


def twiddle(first_index, second_index, total, exponent_sign):
    product = first_index * second_index % total
    return exponent_sign * 2.0 * math.pi / total * product.astype(jnp.float32)


def rotate(values, angles):
    cosines = jnp.cos(angles)
    sines = jnp.sin(angles)
    return jnp.stack(
        [values[0] * cosines - values[1] * sines, values[0] * sines + values[1] * cosines]
    )


def range_transform(signal, exponent_sign):
    pulse_count = signal.shape[1]
    outer_length = BINS // INNER
    folded = signal.reshape(2, pulse_count, outer_length, INNER)
    sectioned = jnp.einsum(
        "pbmn,pmqk->qbkn",
        folded,
        dft_table(outer_length, exponent_sign, outer_length ** (-0.5)),
        preferred_element_type=jnp.float32,
    )
    angles = twiddle(
        jnp.arange(outer_length, dtype=jnp.int32)[:, None],
        jnp.arange(INNER, dtype=jnp.int32)[None, :],
        BINS,
        exponent_sign,
    )
    sectioned = rotate(sectioned, angles).astype(jnp.bfloat16)
    result = jnp.einsum(
        "pbkn,pnqj->qbjk",
        sectioned,
        dft_table(INNER, exponent_sign, INNER ** (-0.5)),
        preferred_element_type=jnp.float32,
    )
    return result.reshape(2, pulse_count, BINS)


def migrate(padded, first_bin, doppler_index, range_scale, doppler_curve, fm_rate, kernels):
    bin_count = padded.shape[1] - 2 * HALO
    column_count = padded.shape[2]
    scales = lax.dynamic_slice_in_dim(range_scale, first_bin, bin_count)
    rates = lax.dynamic_slice_in_dim(fm_rate, first_bin, bin_count)
    curves = doppler_curve[doppler_index]
    eighths = scales[:, None] * curves[None, :] // 4096
    cell_shift = eighths // 8
    phase_index = eighths - 8 * cell_shift
    tap_weights = []
    for tap_index in range(TAPS):
        weight = jnp.full((bin_count, column_count), kernels[0, tap_index], jnp.float32)
        for phase_level in range(1, PHASES):
            weight = jnp.where(phase_index == phase_level, kernels[phase_level, tap_index], weight)
        tap_weights.append(weight)
    summed = jnp.zeros((2, bin_count, column_count), jnp.float32)
    for offset in range(-HALO, HALO + 1):
        wanted = offset + 3 - cell_shift
        weight = jnp.zeros((bin_count, column_count), jnp.float32)
        for tap_index in range(TAPS):
            weight = jnp.where(wanted == tap_index, tap_weights[tap_index], weight)
        window = padded[:, HALO + offset : HALO + offset + bin_count, :]
        summed = summed + weight[None] * window.astype(jnp.float32)
    signed = (doppler_index + PULSES // 2) % PULSES - PULSES // 2
    square = (signed * signed).astype(jnp.float32)
    angles = jnp.pi * rates[:, None] * square[None, :]
    return rotate(summed, angles).astype(jnp.bfloat16)


def shards(echoes, chirp_spectrum, fm_rate, range_scale, doppler_curve, kernels):
    spectrum = range_transform(echoes, -1.0)
    real_part = spectrum[0] * chirp_spectrum[0][None, :] - spectrum[1] * chirp_spectrum[1][None, :]
    imag_part = spectrum[0] * chirp_spectrum[1][None, :] + spectrum[1] * chirp_spectrum[0][None, :]
    spectrum = jnp.stack([real_part, imag_part]).astype(jnp.bfloat16)
    compressed = range_transform(spectrum, 1.0).astype(jnp.bfloat16)
    columns = lax.axis_size("wide")
    wide_index = lax.axis_index("wide")
    narrow_index = lax.axis_index("narrow")
    pulse_rows = echoes.shape[1]
    aperture = PULSES // columns
    turned = lax.all_to_all(compressed, "wide", split_axis=2, concat_axis=1, tiled=True)
    range_count = turned.shape[2]
    by_column = turned.reshape(2, columns, pulse_rows, range_count)
    column_section = jnp.einsum(
        "pcjr,pcqk->qkjr",
        by_column,
        dft_table(columns, -1.0, columns ** (-0.5)),
        preferred_element_type=jnp.float32,
    )
    pulse_index = narrow_index * pulse_rows + jnp.arange(pulse_rows, dtype=jnp.int32)
    angles = twiddle(
        jnp.arange(columns, dtype=jnp.int32)[:, None], pulse_index[None, :], PULSES, -1.0
    )
    column_section = rotate(column_section, angles[:, :, None]).astype(jnp.bfloat16)
    gathered = lax.all_to_all(column_section, "narrow", split_axis=1, concat_axis=2, tiled=True)
    group_size = gathered.shape[1]
    doppler = jnp.einsum(
        "pkar,paqm->qrkm",
        gathered,
        dft_table(aperture, -1.0, aperture ** (-0.5)),
        preferred_element_type=jnp.float32,
    )
    doppler = doppler.astype(jnp.bfloat16).reshape(2, range_count, group_size * aperture)
    doppler_low = narrow_index * group_size + jnp.arange(group_size, dtype=jnp.int32)
    doppler_index = (
        doppler_low[:, None] + columns * jnp.arange(aperture, dtype=jnp.int32)[None, :]
    ).reshape(-1)
    padded = padded_2(doppler, (("wide", 1),), HALO)
    focused = migrate(
        padded,
        wide_index * range_count,
        doppler_index,
        range_scale,
        doppler_curve,
        fm_rate,
        kernels,
    )
    folded = focused.reshape(2, range_count, group_size, aperture)
    second_section = jnp.einsum(
        "prkm,pmqa->qkar",
        folded,
        dft_table(aperture, 1.0, aperture ** (-0.5)),
        preferred_element_type=jnp.float32,
    )
    angles = twiddle(
        doppler_low[:, None], jnp.arange(aperture, dtype=jnp.int32)[None, :], PULSES, 1.0
    )
    second_section = rotate(second_section, angles[:, :, None]).astype(jnp.bfloat16)
    returned = lax.all_to_all(second_section, "narrow", split_axis=3, concat_axis=1, tiled=True)
    image = jnp.einsum(
        "pkar,pkqc->qrca",
        returned,
        dft_table(columns, 1.0, columns ** (-0.5)),
        preferred_element_type=jnp.float32,
    )
    return image.astype(jnp.bfloat16).reshape(2, -1, PULSES)


def solution(mesh):
    in_specs = (P(None, ("wide", "narrow"), None), P(), P(), P(), P(), P())
    out_specs = P(None, ("wide", "narrow"), None)
    return jax.shard_map(shards, mesh=mesh, in_specs=in_specs, out_specs=out_specs, check_vma=False)
```

profile of v0, /device:TPU:1, one launch (start us, length us, event | category | flops | bytes accessed | tf_op | source)
XLA Modules:
  0.0 1719.8 jit_solution(6818153104775827909)
XLA Ops:
  1.7 1.5 copy.75
  6.1 9.2 copy.73
  15.3 24.0 %reshape.2091 = bf16[64,2,4096]{2,1,0:T(2,128)(2,1)} reshape(bf16[16384,2,16]{2,1,0:T(2,128)(2,1)} %bitcast.210) | data formatting | bytes 2097152
  39.3 13.6 all-to-all-start
  53.2 0.7 fusion.110
  53.9 0.7 fusion.109
  54.7 0.7 fusion.108
  55.4 0.7 fusion.111
  56.4 0.8 dynamic_slice.6
  57.2 6.6 gather_fusion
  63.8 45.5 %select_select_fusion = f32[256,1024]{0,1:T(8,128)S(1)} fusion(s32[1024]{0:T(1024)S(1)} %gather_fusion, s32[256]{0:T(256)S(1)} %dynamic_slice.6, f32[]{:T(128)} %bitcast.12, f32[]{:T(128)} %bitcast.11, f32[]{:T(128)} %bitcast.10, f32[]{:T(128)} %bitcast.9, f32[]{:T(128)} %bitcast.8, f32[]{:T(128)} %bitcast.7, f32[]{:T(128)} %bitcast.6, f32[]{:T(128)} %bitcast.5, ...), kind=kLoop, calls=%fused_computation.149 | loop fusion | flops 29622272 | bytes 1053952 | tf_op jit(solution)/shard_map/jit(_where)/select_n | solution.py:103
  109.3 45.5 %select_select_fusion.1 = f32[256,1024]{0,1:T(8,128)S(1)} fusion(s32[1024]{0:T(1024)S(1)} %gather_fusion, s32[256]{0:T(256)S(1)} %dynamic_slice.6, f32[]{:T(128)} %bitcast.12, f32[]{:T(128)} %bitcast.11, f32[]{:T(128)} %bitcast.10, f32[]{:T(128)} %bitcast.9, f32[]{:T(128)} %bitcast.8, f32[]{:T(128)} %bitcast.7, f32[]{:T(128)} %bitcast.6, f32[]{:T(128)} %bitcast.5, ...), kind=kLoop, calls=%fused_computation.150 | loop fusion | flops 29622272 | bytes 1053952 | tf_op jit(solution)/shard_map/jit(_where)/select_n | solution.py:103
  154.9 46.8 %select_select_fusion.10 = f32[256,1024]{0,1:T(8,128)} fusion(s32[1024]{0:T(1024)S(1)} %gather_fusion, s32[256]{0:T(256)S(1)} %dynamic_slice.6, f32[]{:T(128)} %bitcast.12, f32[]{:T(128)} %bitcast.11, f32[]{:T(128)} %bitcast.10, f32[]{:T(128)} %bitcast.9, f32[]{:T(128)} %bitcast.8, f32[]{:T(128)} %bitcast.7, f32[]{:T(128)} %bitcast.6, f32[]{:T(128)} %bitcast.5, ...), kind=kLoop, calls=%fused_computation.159 | loop fusion | flops 29622272 | bytes 1053952 | tf_op jit(solution)/shard_map/jit(_where)/select_n | solution.py:103
  201.6 46.6 %select_select_fusion.11 = f32[256,1024]{0,1:T(8,128)} fusion(s32[1024]{0:T(1024)S(1)} %gather_fusion, s32[256]{0:T(256)S(1)} %dynamic_slice.6, f32[]{:T(128)} %bitcast.12, f32[]{:T(128)} %bitcast.11, f32[]{:T(128)} %bitcast.10, f32[]{:T(128)} %bitcast.9, f32[]{:T(128)} %bitcast.8, f32[]{:T(128)} %bitcast.7, f32[]{:T(128)} %bitcast.6, f32[]{:T(128)} %bitcast.5, ...), kind=kLoop, calls=%fused_computation.160 | loop fusion | flops 29622272 | bytes 1053952 | tf_op jit(solution)/shard_map/jit(_where)/select_n | solution.py:103
  248.3 46.6 %select_select_fusion.12 = f32[256,1024]{0,1:T(8,128)} fusion(s32[1024]{0:T(1024)S(1)} %gather_fusion, s32[256]{0:T(256)S(1)} %dynamic_slice.6, f32[]{:T(128)} %bitcast.12, f32[]{:T(128)} %bitcast.11, f32[]{:T(128)} %bitcast.10, f32[]{:T(128)} %bitcast.9, f32[]{:T(128)} %bitcast.8, f32[]{:T(128)} %bitcast.7, f32[]{:T(128)} %bitcast.6, f32[]{:T(128)} %bitcast.5, ...), kind=kLoop, calls=%fused_computation.161 | loop fusion | flops 29622272 | bytes 1053952 | tf_op jit(solution)/shard_map/jit(_where)/select_n | solution.py:103
  294.9 46.6 %select_select_fusion.13 = f32[256,1024]{0,1:T(8,128)} fusion(s32[1024]{0:T(1024)S(1)} %gather_fusion, s32[256]{0:T(256)S(1)} %dynamic_slice.6, f32[]{:T(128)} %bitcast.12, f32[]{:T(128)} %bitcast.11, f32[]{:T(128)} %bitcast.10, f32[]{:T(128)} %bitcast.9, f32[]{:T(128)} %bitcast.8, f32[]{:T(128)} %bitcast.7, f32[]{:T(128)} %bitcast.6, f32[]{:T(128)} %bitcast.5, ...), kind=kLoop, calls=%fused_computation.162 | loop fusion | flops 29622272 | bytes 1053952 | tf_op jit(solution)/shard_map/jit(_where)/select_n | solution.py:103
  341.5 46.6 %select_select_fusion.14 = f32[256,1024]{0,1:T(8,128)} fusion(s32[1024]{0:T(1024)S(1)} %gather_fusion, s32[256]{0:T(256)S(1)} %dynamic_slice.6, f32[]{:T(128)} %bitcast.12, f32[]{:T(128)} %bitcast.11, f32[]{:T(128)} %bitcast.10, f32[]{:T(128)} %bitcast.9, f32[]{:T(128)} %bitcast.8, f32[]{:T(128)} %bitcast.7, f32[]{:T(128)} %bitcast.6, f32[]{:T(128)} %bitcast.5, ...), kind=kLoop, calls=%fused_computation.163 | loop fusion | flops 29622272 | bytes 1053952 | tf_op jit(solution)/shard_map/jit(_where)/select_n | solution.py:103
  388.1 46.8 %select_select_fusion.15 = f32[256,1024]{0,1:T(8,128)} fusion(s32[1024]{0:T(1024)S(1)} %gather_fusion, s32[256]{0:T(256)S(1)} %dynamic_slice.6, f32[]{:T(128)} %bitcast.12, f32[]{:T(128)} %bitcast.11, f32[]{:T(128)} %bitcast.10, f32[]{:T(128)} %bitcast.9, f32[]{:T(128)} %bitcast.8, f32[]{:T(128)} %bitcast.7, f32[]{:T(128)} %bitcast.6, f32[]{:T(128)} %bitcast.5, ...), kind=kLoop, calls=%fused_computation.164 | loop fusion | flops 29622272 | bytes 1053952 | tf_op jit(solution)/shard_map/jit(_where)/select_n | solution.py:103
  435.0 46.6 %select_select_fusion.16 = f32[256,1024]{0,1:T(8,128)} fusion(s32[1024]{0:T(1024)S(1)} %gather_fusion, s32[256]{0:T(256)S(1)} %dynamic_slice.6, f32[]{:T(128)} %bitcast.12, f32[]{:T(128)} %bitcast.11, f32[]{:T(128)} %bitcast.10, f32[]{:T(128)} %bitcast.9, f32[]{:T(128)} %bitcast.8, f32[]{:T(128)} %bitcast.7, f32[]{:T(128)} %bitcast.6, f32[]{:T(128)} %bitcast.5, ...), kind=kLoop, calls=%fused_computation.165 | loop fusion | flops 29622272 | bytes 1053952 | tf_op jit(solution)/shard_map/jit(_where)/select_n | solution.py:103
  481.6 46.6 %select_select_fusion.17 = f32[256,1024]{0,1:T(8,128)} fusion(s32[1024]{0:T(1024)S(1)} %gather_fusion, s32[256]{0:T(256)S(1)} %dynamic_slice.6, f32[]{:T(128)} %bitcast.12, f32[]{:T(128)} %bitcast.11, f32[]{:T(128)} %bitcast.10, f32[]{:T(128)} %bitcast.9, f32[]{:T(128)} %bitcast.8, f32[]{:T(128)} %bitcast.7, f32[]{:T(128)} %bitcast.6, f32[]{:T(128)} %bitcast.5, ...), kind=kLoop, calls=%fused_computation.166 | loop fusion | flops 29622272 | bytes 1053952 | tf_op jit(solution)/shard_map/jit(_where)/select_n | solution.py:103
  528.2 46.6 %select_select_fusion.18 = f32[256,1024]{0,1:T(8,128)} fusion(s32[1024]{0:T(1024)S(1)} %gather_fusion, s32[256]{0:T(256)S(1)} %dynamic_slice.6, f32[]{:T(128)} %bitcast.12, f32[]{:T(128)} %bitcast.11, f32[]{:T(128)} %bitcast.10, f32[]{:T(128)} %bitcast.9, f32[]{:T(128)} %bitcast.8, f32[]{:T(128)} %bitcast.7, f32[]{:T(128)} %bitcast.6, f32[]{:T(128)} %bitcast.5, ...), kind=kLoop, calls=%fused_computation.167 | loop fusion | flops 29622272 | bytes 1053952 | tf_op jit(solution)/shard_map/jit(_where)/select_n | solution.py:103
  574.9 46.6 %select_select_fusion.19 = f32[256,1024]{0,1:T(8,128)} fusion(s32[1024]{0:T(1024)S(1)} %gather_fusion, s32[256]{0:T(256)S(1)} %dynamic_slice.6, f32[]{:T(128)} %bitcast.12, f32[]{:T(128)} %bitcast.11, f32[]{:T(128)} %bitcast.10, f32[]{:T(128)} %bitcast.9, f32[]{:T(128)} %bitcast.8, f32[]{:T(128)} %bitcast.7, f32[]{:T(128)} %bitcast.6, f32[]{:T(128)} %bitcast.5, ...), kind=kLoop, calls=%fused_computation.168 | loop fusion | flops 29622272 | bytes 1053952 | tf_op jit(solution)/shard_map/jit(_where)/select_n | solution.py:103
  621.5 47.0 %select_select_fusion.2 = f32[256,1024]{0,1:T(8,128)} fusion(s32[1024]{0:T(1024)S(1)} %gather_fusion, s32[256]{0:T(256)S(1)} %dynamic_slice.6, f32[]{:T(128)} %bitcast.12, f32[]{:T(128)} %bitcast.11, f32[]{:T(128)} %bitcast.10, f32[]{:T(128)} %bitcast.9, f32[]{:T(128)} %bitcast.8, f32[]{:T(128)} %bitcast.7, f32[]{:T(128)} %bitcast.6, f32[]{:T(128)} %bitcast.5, ...), kind=kLoop, calls=%fused_computation.151 | loop fusion | flops 29622272 | bytes 1053952 | tf_op jit(solution)/shard_map/jit(_where)/select_n | solution.py:103
  668.5 46.6 %select_select_fusion.20 = f32[256,1024]{0,1:T(8,128)} fusion(s32[1024]{0:T(1024)S(1)} %gather_fusion, s32[256]{0:T(256)S(1)} %dynamic_slice.6, f32[]{:T(128)} %bitcast.12, f32[]{:T(128)} %bitcast.11, f32[]{:T(128)} %bitcast.10, f32[]{:T(128)} %bitcast.9, f32[]{:T(128)} %bitcast.8, f32[]{:T(128)} %bitcast.7, f32[]{:T(128)} %bitcast.6, f32[]{:T(128)} %bitcast.5, ...), kind=kLoop, calls=%fused_computation.169 | loop fusion | flops 29622272 | bytes 1053952 | tf_op jit(solution)/shard_map/jit(_where)/select_n | solution.py:103
  715.1 46.6 %select_select_fusion.21 = f32[256,1024]{0,1:T(8,128)} fusion(s32[1024]{0:T(1024)S(1)} %gather_fusion, s32[256]{0:T(256)S(1)} %dynamic_slice.6, f32[]{:T(128)} %bitcast.12, f32[]{:T(128)} %bitcast.11, f32[]{:T(128)} %bitcast.10, f32[]{:T(128)} %bitcast.9, f32[]{:T(128)} %bitcast.8, f32[]{:T(128)} %bitcast.7, f32[]{:T(128)} %bitcast.6, f32[]{:T(128)} %bitcast.5, ...), kind=kLoop, calls=%fused_computation.170 | loop fusion | flops 29622272 | bytes 1053952 | tf_op jit(solution)/shard_map/jit(_where)/select_n | solution.py:103
  761.8 46.6 %select_select_fusion.22 = f32[256,1024]{0,1:T(8,128)} fusion(s32[1024]{0:T(1024)S(1)} %gather_fusion, s32[256]{0:T(256)S(1)} %dynamic_slice.6, f32[]{:T(128)} %bitcast.12, f32[]{:T(128)} %bitcast.11, f32[]{:T(128)} %bitcast.10, f32[]{:T(128)} %bitcast.9, f32[]{:T(128)} %bitcast.8, f32[]{:T(128)} %bitcast.7, f32[]{:T(128)} %bitcast.6, f32[]{:T(128)} %bitcast.5, ...), kind=kLoop, calls=%fused_computation.171 | loop fusion | flops 29622272 | bytes 1053952 | tf_op jit(solution)/shard_map/jit(_where)/select_n | solution.py:103
  808.4 46.6 %select_select_fusion.23 = f32[256,1024]{0,1:T(8,128)} fusion(s32[1024]{0:T(1024)S(1)} %gather_fusion, s32[256]{0:T(256)S(1)} %dynamic_slice.6, f32[]{:T(128)} %bitcast.12, f32[]{:T(128)} %bitcast.11, f32[]{:T(128)} %bitcast.10, f32[]{:T(128)} %bitcast.9, f32[]{:T(128)} %bitcast.8, f32[]{:T(128)} %bitcast.7, f32[]{:T(128)} %bitcast.6, f32[]{:T(128)} %bitcast.5, ...), kind=kLoop, calls=%fused_computation.172 | loop fusion | flops 29622272 | bytes 1053952 | tf_op jit(solution)/shard_map/jit(_where)/select_n | solution.py:103
  855.0 46.8 %select_select_fusion.24 = f32[256,1024]{0,1:T(8,128)} fusion(s32[1024]{0:T(1024)S(1)} %gather_fusion, s32[256]{0:T(256)S(1)} %dynamic_slice.6, f32[]{:T(128)} %bitcast.12, f32[]{:T(128)} %bitcast.11, f32[]{:T(128)} %bitcast.10, f32[]{:T(128)} %bitcast.9, f32[]{:T(128)} %bitcast.8, f32[]{:T(128)} %bitcast.7, f32[]{:T(128)} %bitcast.6, f32[]{:T(128)} %bitcast.5, ...), kind=kLoop, calls=%fused_computation.173 | loop fusion | flops 29622272 | bytes 1053952 | tf_op jit(solution)/shard_map/jit(_where)/select_n | solution.py:103
  901.8 46.6 %select_select_fusion.25 = f32[256,1024]{0,1:T(8,128)} fusion(s32[1024]{0:T(1024)S(1)} %gather_fusion, s32[256]{0:T(256)S(1)} %dynamic_slice.6, f32[]{:T(128)} %bitcast.12, f32[]{:T(128)} %bitcast.11, f32[]{:T(128)} %bitcast.10, f32[]{:T(128)} %bitcast.9, f32[]{:T(128)} %bitcast.8, f32[]{:T(128)} %bitcast.7, f32[]{:T(128)} %bitcast.6, f32[]{:T(128)} %bitcast.5, ...), kind=kLoop, calls=%fused_computation.174 | loop fusion | flops 29622272 | bytes 1053952 | tf_op jit(solution)/shard_map/jit(_where)/select_n | solution.py:103
  948.4 46.6 %select_select_fusion.26 = f32[256,1024]{0,1:T(8,128)} fusion(s32[1024]{0:T(1024)S(1)} %gather_fusion, s32[256]{0:T(256)S(1)} %dynamic_slice.6, f32[]{:T(128)} %bitcast.12, f32[]{:T(128)} %bitcast.11, f32[]{:T(128)} %bitcast.10, f32[]{:T(128)} %bitcast.9, f32[]{:T(128)} %bitcast.8, f32[]{:T(128)} %bitcast.7, f32[]{:T(128)} %bitcast.6, f32[]{:T(128)} %bitcast.5, ...), kind=kLoop, calls=%fused_computation.175 | loop fusion | flops 29622272 | bytes 1053952 | tf_op jit(solution)/shard_map/jit(_where)/select_n | solution.py:103
  995.1 46.6 %select_select_fusion.27 = f32[256,1024]{0,1:T(8,128)} fusion(s32[1024]{0:T(1024)S(1)} %gather_fusion, s32[256]{0:T(256)S(1)} %dynamic_slice.6, f32[]{:T(128)} %bitcast.12, f32[]{:T(128)} %bitcast.11, f32[]{:T(128)} %bitcast.10, f32[]{:T(128)} %bitcast.9, f32[]{:T(128)} %bitcast.8, f32[]{:T(128)} %bitcast.7, f32[]{:T(128)} %bitcast.6, f32[]{:T(128)} %bitcast.5, ...), kind=kLoop, calls=%fused_computation.176 | loop fusion | flops 29622272 | bytes 1053952 | tf_op jit(solution)/shard_map/jit(_where)/select_n | solution.py:103
  1041.7 46.6 %select_select_fusion.28 = f32[256,1024]{0,1:T(8,128)} fusion(s32[1024]{0:T(1024)S(1)} %gather_fusion, s32[256]{0:T(256)S(1)} %dynamic_slice.6, f32[]{:T(128)} %bitcast.12, f32[]{:T(128)} %bitcast.11, f32[]{:T(128)} %bitcast.10, f32[]{:T(128)} %bitcast.9, f32[]{:T(128)} %bitcast.8, f32[]{:T(128)} %bitcast.7, f32[]{:T(128)} %bitcast.6, f32[]{:T(128)} %bitcast.5, ...), kind=kLoop, calls=%fused_computation.177 | loop fusion | flops 29622272 | bytes 1053952 | tf_op jit(solution)/shard_map/jit(_where)/select_n | solution.py:103
  1088.3 46.8 %select_select_fusion.29 = f32[256,1024]{0,1:T(8,128)} fusion(s32[1024]{0:T(1024)S(1)} %gather_fusion, s32[256]{0:T(256)S(1)} %dynamic_slice.6, f32[]{:T(128)} %bitcast.12, f32[]{:T(128)} %bitcast.11, f32[]{:T(128)} %bitcast.10, f32[]{:T(128)} %bitcast.9, f32[]{:T(128)} %bitcast.8, f32[]{:T(128)} %bitcast.7, f32[]{:T(128)} %bitcast.6, f32[]{:T(128)} %bitcast.5, ...), kind=kLoop, calls=%fused_computation.178 | loop fusion | flops 29622272 | bytes 1053952 | tf_op jit(solution)/shard_map/jit(_where)/select_n | solution.py:103
  1135.1 46.6 %select_select_fusion.3 = f32[256,1024]{0,1:T(8,128)} fusion(s32[1024]{0:T(1024)S(1)} %gather_fusion, s32[256]{0:T(256)S(1)} %dynamic_slice.6, f32[]{:T(128)} %bitcast.12, f32[]{:T(128)} %bitcast.11, f32[]{:T(128)} %bitcast.10, f32[]{:T(128)} %bitcast.9, f32[]{:T(128)} %bitcast.8, f32[]{:T(128)} %bitcast.7, f32[]{:T(128)} %bitcast.6, f32[]{:T(128)} %bitcast.5, ...), kind=kLoop, calls=%fused_computation.152 | loop fusion | flops 29622272 | bytes 1053952 | tf_op jit(solution)/shard_map/jit(_where)/select_n | solution.py:103
  1181.7 46.6 %select_select_fusion.30 = f32[256,1024]{0,1:T(8,128)} fusion(s32[1024]{0:T(1024)S(1)} %gather_fusion, s32[256]{0:T(256)S(1)} %dynamic_slice.6, f32[]{:T(128)} %bitcast.12, f32[]{:T(128)} %bitcast.11, f32[]{:T(128)} %bitcast.10, f32[]{:T(128)} %bitcast.9, f32[]{:T(128)} %bitcast.8, f32[]{:T(128)} %bitcast.7, f32[]{:T(128)} %bitcast.6, f32[]{:T(128)} %bitcast.5, ...), kind=kLoop, calls=%fused_computation.179 | loop fusion | flops 29622272 | bytes 1053952 | tf_op jit(solution)/shard_map/jit(_where)/select_n | solution.py:103
  1228.4 46.6 %select_select_fusion.31 = f32[256,1024]{0,1:T(8,128)} fusion(s32[1024]{0:T(1024)S(1)} %gather_fusion, s32[256]{0:T(256)S(1)} %dynamic_slice.6, f32[]{:T(128)} %bitcast.12, f32[]{:T(128)} %bitcast.11, f32[]{:T(128)} %bitcast.10, f32[]{:T(128)} %bitcast.9, f32[]{:T(128)} %bitcast.8, f32[]{:T(128)} %bitcast.7, f32[]{:T(128)} %bitcast.6, f32[]{:T(128)} %bitcast.5, ...), kind=kLoop, calls=%fused_computation.180 | loop fusion | flops 29622272 | bytes 1053952 | tf_op jit(solution)/shard_map/jit(_where)/select_n | solution.py:103
  1275.0 46.6 %select_select_fusion.32 = f32[256,1024]{0,1:T(8,128)} fusion(s32[1024]{0:T(1024)S(1)} %gather_fusion, s32[256]{0:T(256)S(1)} %dynamic_slice.6, f32[]{:T(128)} %bitcast.12, f32[]{:T(128)} %bitcast.11, f32[]{:T(128)} %bitcast.10, f32[]{:T(128)} %bitcast.9, f32[]{:T(128)} %bitcast.8, f32[]{:T(128)} %bitcast.7, f32[]{:T(128)} %bitcast.6, f32[]{:T(128)} %bitcast.5, ...), kind=kLoop, calls=%fused_computation.189 | loop fusion | flops 29622272 | bytes 1053952 | tf_op jit(solution)/shard_map/jit(_where)/select_n | solution.py:103
  1321.6 47.0 %select_select_fusion.4 = f32[256,1024]{0,1:T(8,128)} fusion(s32[1024]{0:T(1024)S(1)} %gather_fusion, s32[256]{0:T(256)S(1)} %dynamic_slice.6, f32[]{:T(128)} %bitcast.12, f32[]{:T(128)} %bitcast.11, f32[]{:T(128)} %bitcast.10, f32[]{:T(128)} %bitcast.9, f32[]{:T(128)} %bitcast.8, f32[]{:T(128)} %bitcast.7, f32[]{:T(128)} %bitcast.6, f32[]{:T(128)} %bitcast.5, ...), kind=kLoop, calls=%fused_computation.153 | loop fusion | flops 29622272 | bytes 1053952 | tf_op jit(solution)/shard_map/jit(_where)/select_n | solution.py:103
  1368.6 46.6 %select_select_fusion.5 = f32[256,1024]{0,1:T(8,128)} fusion(s32[1024]{0:T(1024)S(1)} %gather_fusion, s32[256]{0:T(256)S(1)} %dynamic_slice.6, f32[]{:T(128)} %bitcast.12, f32[]{:T(128)} %bitcast.11, f32[]{:T(128)} %bitcast.10, f32[]{:T(128)} %bitcast.9, f32[]{:T(128)} %bitcast.8, f32[]{:T(128)} %bitcast.7, f32[]{:T(128)} %bitcast.6, f32[]{:T(128)} %bitcast.5, ...), kind=kLoop, calls=%fused_computation.154 | loop fusion | flops 29622272 | bytes 1053952 | tf_op jit(solution)/shard_map/jit(_where)/select_n | solution.py:103
  1415.2 46.6 %select_select_fusion.6 = f32[256,1024]{0,1:T(8,128)} fusion(s32[1024]{0:T(1024)S(1)} %gather_fusion, s32[256]{0:T(256)S(1)} %dynamic_slice.6, f32[]{:T(128)} %bitcast.12, f32[]{:T(128)} %bitcast.11, f32[]{:T(128)} %bitcast.10, f32[]{:T(128)} %bitcast.9, f32[]{:T(128)} %bitcast.8, f32[]{:T(128)} %bitcast.7, f32[]{:T(128)} %bitcast.6, f32[]{:T(128)} %bitcast.5, ...), kind=kLoop, calls=%fused_computation.155 | loop fusion | flops 29622272 | bytes 1053952 | tf_op jit(solution)/shard_map/jit(_where)/select_n | solution.py:103
  1462.4 46.6 %select_select_fusion.7 = f32[256,1024]{0,1:T(8,128)} fusion(s32[1024]{0:T(1024)S(1)} %gather_fusion, s32[256]{0:T(256)S(1)} %dynamic_slice.6, f32[]{:T(128)} %bitcast.12, f32[]{:T(128)} %bitcast.11, f32[]{:T(128)} %bitcast.10, f32[]{:T(128)} %bitcast.9, f32[]{:T(128)} %bitcast.8, f32[]{:T(128)} %bitcast.7, f32[]{:T(128)} %bitcast.6, f32[]{:T(128)} %bitcast.5, ...), kind=kLoop, calls=%fused_computation.156 | loop fusion | flops 29622272 | bytes 1053952 | tf_op jit(solution)/shard_map/jit(_where)/select_n | solution.py:103
  1509.0 46.6 %select_select_fusion.8 = f32[256,1024]{0,1:T(8,128)} fusion(s32[1024]{0:T(1024)S(1)} %gather_fusion, s32[256]{0:T(256)S(1)} %dynamic_slice.6, f32[]{:T(128)} %bitcast.12, f32[]{:T(128)} %bitcast.11, f32[]{:T(128)} %bitcast.10, f32[]{:T(128)} %bitcast.9, f32[]{:T(128)} %bitcast.8, f32[]{:T(128)} %bitcast.7, f32[]{:T(128)} %bitcast.6, f32[]{:T(128)} %bitcast.5, ...), kind=kLoop, calls=%fused_computation.157 | loop fusion | flops 29622272 | bytes 1053952 | tf_op jit(solution)/shard_map/jit(_where)/select_n | solution.py:103
  1555.7 7.8 reshape.2092
  1563.4 11.8 copy.74
  1576.2 1.6 copy.44
  1577.8 5.1 all-to-all-start.1
  1582.9 46.7 %select_select_fusion.9 = f32[256,1024]{0,1:T(8,128)} fusion(s32[1024]{0:T(1024)S(1)} %gather_fusion, s32[256]{0:T(256)S(1)} %dynamic_slice.6, f32[]{:T(128)} %bitcast.12, f32[]{:T(128)} %bitcast.11, f32[]{:T(128)} %bitcast.10, f32[]{:T(128)} %bitcast.9, f32[]{:T(128)} %bitcast.8, f32[]{:T(128)} %bitcast.7, f32[]{:T(128)} %bitcast.6, f32[]{:T(128)} %bitcast.5, ...), kind=kLoop, calls=%fused_computation.158 | loop fusion | flops 29622272 | bytes 1053952 | tf_op jit(solution)/shard_map/jit(_where)/select_n | solution.py:103
  1629.6 1.5 copy.45
  1631.9 3.4 collective-permute-start
  1635.3 1.3 collective-permute-start.1
  1636.6 0.8 dynamic-slice_multiply_fusion
  1637.3 9.2 collective-permute-done
  1646.5 3.8 collective-permute-done.1
  1650.4 21.8 %multiply_add_fusion = f32[2,256,1024]{1,2,0:T(8,128)S(1)} fusion(bf16[2,256,1024]{1,2,0:T(8,128)(2,1)S(1)} %bitcast.213, bf16[2,16,1024]{1,2,0:T(8,128)(2,1)S(1)} %collective-permute-done.1, bf16[2,16,1024]{1,2,0:T(8,128)(2,1)S(1)} %collective-permute-done, f32[256,1024]{0,1:T(8,128)S(1)} %select_select_fusion, f32[256,1024]{0,1:T(8,128)S(1)} %select_select_fusion.1, ...), kind=kLoop, calls=%fused_computation.68 | loop fusion | flops 101711872 | bytes 37879808 | tf_op jit(solution)/shard_map/add | solution.py:105
  1672.2 4.7 fusion.7
  1676.9 0.5 convolution_bitcast_fusion
  1677.9 3.1 copy.47
  1680.9 1.7 reshape.2093
  1682.6 20.5 %all_to_all.51 = bf16[4,2,65536]{2,1,0:T(2,128)(2,1)S(1)} all-to-all(bf16[4,2,65536]{2,1,0:T(2,128)(2,1)S(1)} %reshape.2093), channel_id=1, replica_groups=mesh['wide'=64,'narrow'=4] {'narrow'}, dimensions={0} | all-to-all | bytes 2097152 | tf_op jit(solution)/shard_map/all_to_all | solution.py:171
  1703.1 2.7 reshape.2094
  1705.8 5.2 copy.48
  1711.1 2.1 fusion
  1713.2 3.9 copy.50
  1717.1 2.5 reshape.2060
  (63 shorter events, 7.8 us)
Async XLA Ops:
  0.0 57.2 %copy-start = (s32[4096]{0:T(1024)S(1)}, s32[4096]{0:T(1024)}, u32[]{:S(2)}) copy-start(s32[4096]{0:T(1024)} %param.10) | copy-start | bytes 49156
  0.0 3.1 copy-start.10
  39.3 14.0 copy-start.9
  39.3 1516.4 %all-to-all-start = ((bf16[64,2,4096]{2,1,0:T(2,128)(2,1)}), bf16[64,2,4096]{2,1,0:T(2,128)(2,1)S(1)}, u32[]{:S(2)}, u32[]{:S(2)}) async-start(bf16[64,2,4096]{2,1,0:T(2,128)(2,1)} %reshape.2091), calls=%async_computation | async-start | bytes 2097152 | tf_op jit(solution)/shard_map/all_to_all | solution.py:123
  1577.8 51.9 %all-to-all-start.1 = ((bf16[2,64,16,256]{3,2,0,1:T(8,128)(2,1)}), bf16[2,64,16,256]{3,2,0,1:T(8,128)(2,1)}, u32[]{:S(2)}, u32[]{:S(2)}) async-start(bf16[2,64,16,256]{3,2,0,1:T(8,128)(2,1)} %copy.44), calls=%async_computation.1 | async-start | bytes 2097152 | tf_op jit(solution)/shard_map/all_to_all | solution.py:137
  1582.9 67.4 %copy-start.8 = (f32[256,1024]{0,1:T(8,128)S(1)}, f32[256,1024]{0,1:T(8,128)}, u32[]{:S(2)}) copy-start(f32[256,1024]{0,1:T(8,128)} %select_select_fusion.16) | copy-start | bytes 3145732
  1629.6 20.7 %copy-start.6 = (f32[256,1024]{0,1:T(8,128)S(1)}, f32[256,1024]{0,1:T(8,128)}, u32[]{:S(2)}) copy-start(f32[256,1024]{0,1:T(8,128)} %select_select_fusion.14) | copy-start | bytes 3145732
  1629.6 20.7 %copy-start.7 = (f32[256,1024]{0,1:T(8,128)S(1)}, f32[256,1024]{0,1:T(8,128)}, u32[]{:S(2)}) copy-start(f32[256,1024]{0,1:T(8,128)} %select_select_fusion.15) | copy-start | bytes 3145732
  1631.1 19.2 %copy-start.2 = (f32[256,1024]{0,1:T(8,128)S(1)}, f32[256,1024]{0,1:T(8,128)}, u32[]{:S(2)}) copy-start(f32[256,1024]{0,1:T(8,128)} %select_select_fusion.10) | copy-start | bytes 3145732
  1631.1 19.2 %copy-start.3 = (f32[256,1024]{0,1:T(8,128)S(1)}, f32[256,1024]{0,1:T(8,128)}, u32[]{:S(2)}) copy-start(f32[256,1024]{0,1:T(8,128)} %select_select_fusion.11) | copy-start | bytes 3145732
  1631.2 19.2 %copy-start.4 = (f32[256,1024]{0,1:T(8,128)S(1)}, f32[256,1024]{0,1:T(8,128)}, u32[]{:S(2)}) copy-start(f32[256,1024]{0,1:T(8,128)} %select_select_fusion.12) | copy-start | bytes 3145732
  1631.2 19.2 %copy-start.5 = (f32[256,1024]{0,1:T(8,128)S(1)}, f32[256,1024]{0,1:T(8,128)}, u32[]{:S(2)}) copy-start(f32[256,1024]{0,1:T(8,128)} %select_select_fusion.13) | copy-start | bytes 3145732
  1631.9 14.6 collective-permute-start
  1635.3 15.1 collective-permute-start.1
  1713.2 6.4 copy-start.1
where the time goes:
time: 1750 us; the launch traced here: 1720 us
  other arithmetic  1570 us (90%)
  local copies, waits for them, and re-layouts  87 us (5%)
  starting transfers between devices  23.4 us (1%)
  blocking collectives  20.5 us (1%)
    select_n x33, other arithmetic, migrate(): weight = jnp.where(wanted == tap_index, tap_weights[tap_index], weight)  1540 us
    unnamed x27, local copies, waits for them, and re-layouts  37.6 us
  transfers between devices with their start and end apart: 4, of which 2 were waited for; matrix products, arithmetic and copies ran while one was open for 90% of the time, Pallas kernels for 0%

commit v1 on v0

v1 whole, which is shorter than its diff:
```python
import functools
import math

import jax
import jax.numpy as jnp
import ml_dtypes
import numpy as np
from jax import lax
from jax.experimental import pallas as pl
from jax.experimental.pallas import tpu as pltpu
from jax.sharding import PartitionSpec as P

PULSES = 4096
BINS = 16384
EDGE = 128
LOW = 32
TAPS = 8
PHASES = 8
HALO = 16
DEVICES = 256
OWN = BINS // DEVICES
ROWS = PULSES // DEVICES
AXES = ("wide", "narrow")
F32 = jnp.float32
BF16 = jnp.bfloat16


def roots(product, total):
    angles = 2.0 * np.pi / total * (product % total)
    return np.cos(angles), np.sin(angles)


def range_tables():
    count = np.arange(EDGE)
    c, s = roots(np.outer(count, count), EDGE)
    c, s = c / math.sqrt(EDGE), s / math.sqrt(EDGE)
    fwd_left = np.block([[c, s], [-s, c]])
    inv_left = np.block([[c, -s], [s, c]])
    tables = np.stack([fwd_left, fwd_left.T, inv_left.T, inv_left])
    tc, ts = roots(np.outer(count, count), BINS)
    return tables.astype(ml_dtypes.bfloat16), np.stack([tc, ts]).astype(np.float32)


def azimuth_tables():
    low = np.arange(LOW)[:, None, None]
    n = np.arange(EDGE)[None, :, None]
    j = np.arange(EDGE)[None, None, :]
    c, s = roots(n * (low + LOW * j), PULSES)
    return (np.stack([c, s], axis=1) / math.sqrt(PULSES)).astype(ml_dtypes.bfloat16)


def fft(values, sign):
    count = len(values)
    if count == 1:
        return values
    even, odd = fft(values[0::2], sign), fft(values[1::2], sign)
    half = count // 2
    out = [None] * count
    for k in range(half):
        (ar, ai), (br, bi) = even[k], odd[k]
        if k == 0:
            tr, ti = br, bi
        elif 4 * k == count:
            tr, ti = (-bi, br) if sign > 0 else (bi, -br)
        else:
            angle = 2.0 * math.pi * k / count
            c, s = math.cos(angle), sign * math.sin(angle)
            if 8 * k == count:
                tr, ti = (br - bi * (1 if sign > 0 else -1)) * c, (bi + br * (1 if sign > 0 else -1)) * c
            else:
                tr, ti = br * c - bi * s, br * s + bi * c
        out[k] = (ar + tr, ai + ti)
        out[k + half] = (ar - tr, ai - ti)
    return out


def dot(a, b):
    return jnp.dot(a, b, preferred_element_type=F32)


def range_kernel(echo_ref, chirp_ref, table_ref, twiddle_ref, send_ref, wide_ref, turned_ref):
    def spread(m, carry):
        columns = pl.ds(pl.multiple_of(m * EDGE, EDGE), EDGE)
        for part in range(2):
            block = echo_ref[part, :, columns].astype(F32)
            wide_ref[part, pl.ds(pl.multiple_of(m * ROWS, ROWS), ROWS), :] = block
        return carry

    lax.fori_loop(0, EDGE, spread, 0, unroll=8)
    tc, ts = twiddle_ref[0], twiddle_ref[1]

    def pair(i, carry):
        b = 2 * i
        signal = jnp.concatenate(
            [
                jnp.concatenate(
                    [wide_ref[part, pl.ds(b + h, EDGE, stride=ROWS), :] for h in range(2)], axis=1
                )
                for part in range(2)
            ],
            axis=0,
        ).astype(BF16)
        first = dot(table_ref[0], signal)
        rows = []
        for h in range(2):
            re, im = first[:EDGE, h * EDGE : (h + 1) * EDGE], first[EDGE:, h * EDGE : (h + 1) * EDGE]
            rows.append(jnp.concatenate([re * tc + im * ts, im * tc - re * ts], axis=1))
        spectrum = dot(jnp.concatenate(rows, axis=0).astype(BF16), table_ref[1])
        rows = []
        for h in range(2):
            re, im = spectrum[h * EDGE : (h + 1) * EDGE, :EDGE], spectrum[h * EDGE : (h + 1) * EDGE, EDGE:]
            rows.append(
                jnp.concatenate(
                    [re * chirp_ref[0] - im * chirp_ref[1], re * chirp_ref[1] + im * chirp_ref[0]], axis=1
                )
            )
        back = dot(jnp.concatenate(rows, axis=0).astype(BF16), table_ref[2])
        columns = []
        for h in range(2):
            re, im = back[h * EDGE : (h + 1) * EDGE, :EDGE], back[h * EDGE : (h + 1) * EDGE, EDGE:]
            columns.append(jnp.concatenate([re * tc - im * ts, im * tc + re * ts], axis=0))
        result = dot(table_ref[3], jnp.concatenate(columns, axis=1).astype(BF16))
        for h in range(2):
            for part in range(2):
                turned_ref[part, pl.ds(b + h, EDGE, stride=ROWS), :] = result[
                    part * EDGE : (part + 1) * EDGE, h * EDGE : (h + 1) * EDGE
                ]
        return carry

    lax.fori_loop(0, ROWS // 2, pair, 0)
    low_half = lax.broadcasted_iota(jnp.int32, (ROWS, EDGE), 1) < EDGE // 2

    def pack(u, carry):
        rows = pl.ds(pl.multiple_of(u * ROWS, ROWS), ROWS)
        re, im = turned_ref[0, rows, :], turned_ref[1, rows, :]
        send_ref[2 * u] = jnp.where(low_half, re, pltpu.roll(im, EDGE // 2, 1)).astype(BF16)
        send_ref[2 * u + 1] = jnp.where(low_half, pltpu.roll(re, EDGE // 2, 1), im).astype(BF16)
        return carry

    lax.fori_loop(0, EDGE, pack, 0, unroll=8)


def compress(echoes, chirp, tables, twiddles):
    return pl.pallas_call(
        range_kernel,
        out_shape=jax.ShapeDtypeStruct((DEVICES, ROWS, EDGE), BF16),
        scratch_shapes=[
            pltpu.VMEM((2, EDGE * ROWS, EDGE), F32),
            pltpu.VMEM((2, EDGE * ROWS, EDGE), F32),
        ],
        compiler_params=pltpu.CompilerParams(vmem_limit_bytes=40 << 20),
        name="compress",
    )(echoes, chirp, tables, twiddles)


def split_pairs(got_ref, re_ref, im_ref):
    half = EDGE // 2
    low_half = lax.broadcasted_iota(jnp.int32, (ROWS, EDGE), 1) < half

    def step(m, carry):
        for g in range(half // ROWS):
            near = got_ref[m * 8 + g].astype(F32)
            far = got_ref[m * 8 + 4 + g].astype(F32)
            rows = pl.ds(g * ROWS, ROWS)
            re_ref[m, rows, :] = jnp.where(low_half, near, pltpu.roll(far, half, 1))
            im_ref[m, rows, :] = jnp.where(low_half, pltpu.roll(near, half, 1), far)
        return carry

    lax.fori_loop(0, LOW, step, 0, unroll=2)


def low_transform(re_ref, im_ref, sign, store):
    def step(g, carry):
        rows = pl.ds(pl.multiple_of(g * 8, 8), 8)
        values = fft([(re_ref[m, rows, :], im_ref[m, rows, :]) for m in range(LOW)], sign)
        for k, (re, im) in enumerate(values):
            store(k, g, re, im)
        return carry

    lax.fori_loop(0, 8, step, 0)


def low_store(re_ref, im_ref):
    def store(k, g, re, im):
        rows = pl.ds(pl.multiple_of(g * 8, 8), 8)
        re_ref[k, rows, :] = re
        im_ref[k, rows, :] = im

    return store


def block_table(table_ref, k):
    c, s = table_ref[k, 0], table_ref[k, 1]
    return jnp.concatenate(
        [jnp.concatenate([c, -s], axis=1), jnp.concatenate([s, c], axis=1)], axis=0
    )


def doppler_kernel(got_ref, table_ref, out_ref, re_ref, im_ref, wide_ref):
    half = EDGE // 2
    split_pairs(got_ref, re_ref, im_ref)
    low_transform(re_ref, im_ref, -1, low_store(re_ref, im_ref))

    def step(k, carry):
        re, im = re_ref[k], im_ref[k]
        left = jnp.concatenate(
            [re, pltpu.roll(re, half, 1), im, pltpu.roll(im, half, 1)], axis=0
        ).astype(BF16)
        result = lax.dot_general(
            left, block_table(table_ref, k), (((0,), (0,)), ((), ())), preferred_element_type=F32
        )
        for part in range(2):
            wide_ref[part, pl.ds(k, OWN, stride=LOW), :] = result[:OWN, part * EDGE : (part + 1) * EDGE]
        return carry

    lax.fori_loop(0, LOW, step, 0)

    def narrow(r, carry):
        rows = pl.ds(pl.multiple_of(r * LOW, LOW), LOW)
        for part in range(2):
            out_ref[part, r] = wide_ref[part, rows, :].astype(BF16)
        return carry

    lax.fori_loop(0, OWN, narrow, 0, unroll=4)


def doppler_spectra(got, table):
    return pl.pallas_call(
        doppler_kernel,
        out_shape=jax.ShapeDtypeStruct((2, OWN, LOW, EDGE), BF16),
        scratch_shapes=[
            pltpu.VMEM((LOW, EDGE // 2, EDGE), F32),
            pltpu.VMEM((LOW, EDGE // 2, EDGE), F32),
            pltpu.VMEM((2, OWN * LOW, EDGE), F32),
        ],
        compiler_params=pltpu.CompilerParams(vmem_limit_bytes=40 << 20),
        name="doppler_spectra",
    )(got, table)


def turn(turns):
    x = turns - jnp.round(turns)
    y = x * x
    c = jnp.full_like(x, COS_TERMS[-1])
    for term in COS_TERMS[-2::-1]:
        c = c * y + term
    s = jnp.full_like(x, SIN_TERMS[-1])
    for term in SIN_TERMS[-2::-1]:
        s = s * y + term
    return c, s * x


def fitted_terms():
    x = np.cos(np.pi * (np.arange(400) + 0.5) / 800) * 0.5
    y = x * x
    powers = np.stack([y**i for i in range(6)], axis=1)
    c = np.linalg.lstsq(powers, np.cos(2 * np.pi * x), rcond=None)[0]
    s = np.linalg.lstsq(powers * x[:, None], np.sin(2 * np.pi * x), rcond=None)[0]
    return [float(v) for v in c], [float(v) for v in s]


COS_TERMS, SIN_TERMS = fitted_terms()


def migrate_rows(r, padded_ref, scale_ref, rate_ref, curve_ref, square_ref, taps_ref, store):
    scale = scale_ref[r]
    negative = scale < 0
    first = r + HALO - 3 - jnp.where(negative, SHIFT_LOW, 0)
    offset = jnp.where(negative, 8.0 * SHIFT_LOW, 0.0).astype(F32)
    scale = scale.astype(F32) * (1.0 / 4096.0)
    for h in range(2):
        rows = pl.ds(16 * h, 16)
        level = (jnp.floor(curve_ref[rows, :] * scale) + offset).astype(BF16)
        bits = []
        for weight in (64, 32, 16, 8, 4, 2, 1):
            bit = level >= jnp.asarray(weight, BF16)
            bits.append(bit)
            if weight > 1:
                level = jnp.where(bit, level - jnp.asarray(weight, BF16), level)
        weights = []
        for t in range(TAPS):
            level4 = [jnp.where(bits[6], taps_ref[(2 * i + 1) * TAPS + t], taps_ref[2 * i * TAPS + t]) for i in range(4)]
            level2 = [jnp.where(bits[5], level4[2 * i + 1], level4[2 * i]) for i in range(2)]
            weights.append(jnp.where(bits[4], level2[1], level2[0]))
        sums = []
        for part in range(2):
            x = [padded_ref[part, first + i, rows, :] for i in range(21)]
            x = [jnp.where(bits[0], x[i + 8], x[i]) if i < 13 else x[i] for i in range(15)]
            x = [jnp.where(bits[1], x[i + 4], x[i]) for i in range(11)]
            x = [jnp.where(bits[2], x[i + 2], x[i]) for i in range(9)]
            x = [jnp.where(bits[3], x[i + 1], x[i]) for i in range(8)]
            terms = [a * b for a, b in zip(x, weights)]
            while len(terms) > 1:
                terms = [terms[i] + terms[i + 1] for i in range(0, len(terms), 2)]
            sums.append(terms[0].astype(F32))
        c, s = turn(square_ref[rows, :] * rate_ref[r])
        store(r, h, sums[0] * c - sums[1] * s, sums[0] * s + sums[1] * c)


SHIFT_LOW = 13


def focus_kernel(
    body_ref, head_ref, tail_ref, scale_ref, rate_ref, curve_ref, square_ref, taps_ref, table_ref,
    image_ref, padded_ref, wide_ref, re_ref, im_ref,
):
    for part in range(2):
        padded_ref[part, 0:HALO] = head_ref[part]
        padded_ref[part, HALO : HALO + OWN] = body_ref[part]
        padded_ref[part, HALO + OWN : 2 * HALO + OWN] = tail_ref[part]

    def store(r, h, re, im):
        rows = pl.ds(pl.multiple_of(r * LOW + 16 * h, 16), 16)
        wide_ref[0, rows, :] = re
        wide_ref[1, rows, :] = im

    def step(r, carry):
        migrate_rows(r, padded_ref, scale_ref, rate_ref, curve_ref, square_ref, taps_ref, store)
        return carry

    lax.fori_loop(0, OWN, step, 0)

    def back(k, carry):
        left = jnp.concatenate(
            [wide_ref[part, pl.ds(k, OWN, stride=LOW), :] for part in range(2)], axis=1
        ).astype(BF16)
        result = lax.dot_general(
            left, block_table(table_ref, k), (((1,), (1,)), ((), ())), preferred_element_type=F32
        )
        re_ref[k] = result[:, :EDGE]
        im_ref[k] = result[:, EDGE:]
        return carry

    lax.fori_loop(0, LOW, back, 0)
    low_transform(re_ref, im_ref, 1, low_store(re_ref, im_ref))

    def final(h, carry):
        columns = pl.ds(pl.multiple_of(h * EDGE, EDGE), EDGE)
        image_ref[0, :, columns] = re_ref[h].astype(BF16)
        image_ref[1, :, columns] = im_ref[h].astype(BF16)
        return carry

    lax.fori_loop(0, LOW, final, 0)


def focus(body, head, tail, scales, rates, curve, square, taps, table):
    vmem, smem = pl.BlockSpec(memory_space=pltpu.VMEM), pl.BlockSpec(memory_space=pltpu.SMEM)
    return pl.pallas_call(
        focus_kernel,
        out_shape=jax.ShapeDtypeStruct((2, OWN, PULSES), BF16),
        in_specs=[vmem, vmem, vmem, smem, smem, vmem, vmem, vmem, vmem],
        out_specs=vmem,
        scratch_shapes=[
            pltpu.VMEM((2, 2 * HALO + OWN + 8, LOW, EDGE), BF16),
            pltpu.VMEM((2, OWN * LOW, EDGE), F32),
            pltpu.VMEM((LOW, OWN, EDGE), F32),
            pltpu.VMEM((LOW, OWN, EDGE), F32),
        ],
        compiler_params=pltpu.CompilerParams(vmem_limit_bytes=48 << 20),
        name="focus",
    )(body, head, tail, scales, rates, curve, square, taps, table)


def shards(echoes, chirp_spectrum, fm_rate, range_scale, doppler_curve, kernels):
    me = lax.axis_index("wide") * lax.axis_size("narrow") + lax.axis_index("narrow")
    tables, twiddles = range_tables()
    azimuth = jnp.asarray(azimuth_tables())
    chirp = chirp_spectrum.reshape(2, EDGE, EDGE).transpose(0, 2, 1)
    send = compress(echoes, chirp, jnp.asarray(tables), jnp.asarray(twiddles))
    got = lax.all_to_all(send, AXES, 0, 0, tiled=True)
    body = doppler_spectra(got, azimuth)
    head = lax.ppermute(body[:, OWN - HALO :], AXES, [(i, i + 1) for i in range(DEVICES - 1)])
    tail = lax.ppermute(body[:, :HALO], AXES, [(i + 1, i) for i in range(DEVICES - 1)])
    scales = lax.dynamic_slice_in_dim(range_scale, me * OWN, OWN)
    rates = lax.dynamic_slice_in_dim(fm_rate, me * OWN, OWN) * 0.5
    curve = doppler_curve.astype(F32).reshape(EDGE, LOW).T
    index = np.arange(PULSES)
    signed = (index + PULSES // 2) % PULSES - PULSES // 2
    square = jnp.asarray((signed * signed).astype(np.float32).reshape(EDGE, LOW).T)
    taps = jnp.broadcast_to(kernels.reshape(-1, 1, 1).astype(BF16), (PHASES * TAPS, 16, EDGE))
    return focus(body, head, tail, scales, rates, curve, square, taps, azimuth)


def solution(mesh):
    in_specs = (P(None, AXES, None), P(), P(), P(), P(), P())
    out_specs = P(None, AXES, None)
    return jax.shard_map(shards, mesh=mesh, in_specs=in_specs, out_specs=out_specs, check_vma=False)
```

time: 1750 us -> 104 us (0.06)
  the two profiles are of different devices: /device:TPU:1 before, /device:TPU:32 now
where the time goes in v1:
time: 104 us; the launch traced here: 103 us
  blocking collectives  44.4 us (43%)
  Pallas kernels  35.6 us (34%)
  waiting for transfers between devices  8.78 us (8%)
  starting transfers between devices  7.63 us (7%)
  local copies, waits for them, and re-layouts  6.15 us (6%)
    all_to_all x1, blocking collectives, shards(): got = lax.all_to_all(send, AXES, 0, 0, tiled=True)  44.4 us
    pallas_call x1, Pallas kernels, focus(): pl.pallas_call(focus_kernel, out_shape=jax.ShapeDtypeStruct((2, OWN, PULS...  15.6 us
    pallas_call x1, Pallas kernels, doppler_spectra(): pl.pallas_call(doppler_kernel, out_shape=jax.ShapeDtypeStruct((2, OWN, LO...  12.1 us
    ppermute x1, waiting for transfers between devices, shards(): lax.ppermute(body[:, OWN - HALO:], AXES, [(i, i + 1) for i in range(DEVIC...  8.34 us
    pallas_call x1, Pallas kernels, compress(): pl.pallas_call(range_kernel, out_shape=jax.ShapeDtypeStruct((DEVICES, ROW...  7.87 us
    ppermute x1, starting transfers between devices, shards(): lax.ppermute(body[:, :HALO], AXES, [(i + 1, i) for i in range(DEVICES - 1)])  5.71 us
    unnamed x15, local copies, waits for them, and re-layouts  4.09 us
  transfers between devices with their start and end apart: 2, of which 2 were waited for; matrix products, arithmetic and copies ran while one was open for 2% of the time, Pallas kernels for 0%

profile of v1, /device:TPU:32, one launch (start us, length us, event | category | flops | bytes accessed | tf_op | source)
XLA Modules:
  0.0 103.4 jit_solution(16963295460740854587)
XLA Ops:
  0.0 0.9 copy.15
  0.9 0.1 copy.11
  1.0 0.0 copy-start.1
  1.0 1.2 %copy-done.1 = bf16[2,16,16384]{2,1,0:T(8,128)(2,1)S(1)} copy-done((bf16[2,16,16384]{2,1,0:T(8,128)(2,1)S(1)}, bf16[2,16,16384]{2,1,0:T(8,128)(2,1)}, u32[]{:S(2)}) %copy-start.1) | copy-done | bytes 1048600
  2.2 0.0 copy-start.2
  2.2 1.0 %copy-done.2 = bf16[4,256,256]{2,1,0:T(8,128)(2,1)S(1)} copy-done((bf16[4,256,256]{2,1,0:T(8,128)(2,1)S(1)}, bf16[4,256,256]{2,1,0:T(8,128)(2,1)}, u32[]{:S(2)}) %copy-start.2) | copy-done | bytes 524312
  3.3 0.0 copy-start.3
  3.3 0.9 copy-done.3
  4.2 0.0 copy-start
  4.2 7.9 %compress.1 = bf16[256,16,128]{2,1,0:T(8,128)(2,1)S(1)} custom-call(bf16[2,16,16384]{2,1,0:T(8,128)(2,1)S(1)} %copy-done.1, f32[2,128,128]{2,1,0:T(8,128)S(1)} %bitcast.6, bf16[4,256,256]{2,1,0:T(8,128)(2,1)S(1)} %copy-done.2, f32[2,128,128]{2,1,0:T(8,128)S(1)} %copy-done.3), custom_call_target="tpu_custom_call" | custom-call | tf_op jit(solution)/shard_map/compress/pallas_call | solution.py:144
  12.1 44.4 %all_to_all.5.got_ref = bf16[256,16,128]{2,1,0:T(8,128)(2,1)S(1)} all-to-all(bf16[256,16,128]{2,1,0:T(8,128)(2,1)S(1)} %compress.1), channel_id=1, replica_groups=mesh['wide'=64,'narrow'=4] {'wide','narrow'}, dimensions={0} | all-to-all | bytes 2097152 | tf_op jit(solution)/shard_map/all_to_all | solution.py:370
  56.4 0.0 copy-done
  56.4 0.0 copy-start.6
  56.5 0.0 copy-start.5
  56.5 0.0 copy-start.4
  56.5 12.1 %doppler_spectra.1.body_ref = bf16[2,64,32,128]{3,2,1,0:T(8,128)(2,1)S(1)} custom-call(bf16[256,16,128]{2,1,0:T(8,128)(2,1)S(1)} %all_to_all.5.got_ref, bf16[32,2,128,128]{3,2,1,0:T(8,128)(2,1)S(1)} %copy-done), custom_call_target="tpu_custom_call" | custom-call | tf_op jit(solution)/shard_map/doppler_spectra/pallas_call | solution.py:228
  68.5 0.8 fusion
  69.3 5.7 %collective-permute-start.1 = (bf16[2,16,32,128]{3,2,1,0:T(8,128)(2,1)}, bf16[2,16,32,128]{3,2,1,0:T(8,128)(2,1)S(1)}, u32[]{:S(2)}, u32[]{:S(2)}) collective-permute-start(bf16[2,16,32,128]{3,2,1,0:T(8,128)(2,1)} %get-tuple-element.5), channel_id=1, source_target_pairs={{1,0},{2,1},{3,2},{4,3},{5,4},{6,5},{7,6},{8,7},{9,8},{10,9},{11,1... | collective-permute-start | bytes 786440 | tf_op jit(solution)/shard_map/ppermute | solution.py:373
  75.1 1.9 %collective-permute-start = (bf16[2,16,32,128]{3,2,1,0:T(8,128)(2,1)}, bf16[2,16,32,128]{3,2,1,0:T(8,128)(2,1)}, u32[]{:S(2)}, u32[]{:S(2)}) collective-permute-start(bf16[2,16,32,128]{3,2,1,0:T(8,128)(2,1)} %get-tuple-element.6), channel_id=1, source_target_pairs={{0,1},{1,2},{2,3},{3,4},{4,5},{5,6},{6,7},{7,8},{8,9},{9,10},{10,1... | collective-permute-start | bytes 786440 | tf_op jit(solution)/shard_map/ppermute | solution.py:372
  77.0 0.0 copy-done.6
  77.0 0.1 convert_element_type.16
  77.1 0.0 copy-done.5
  77.1 0.1 reshape.16
  77.2 0.1 copy.12
  77.3 0.8 dynamic_slice.6.scale_ref
  78.0 0.8 dynamic-slice_multiply_fusion.rate_ref
  78.8 0.4 collective-permute-done.1.tail_ref
  79.2 8.3 %collective-permute-done.head_ref = bf16[2,16,32,128]{3,2,1,0:T(8,128)(2,1)} collective-permute-done((bf16[2,16,32,128]{3,2,1,0:T(8,128)(2,1)}, bf16[2,16,32,128]{3,2,1,0:T(8,128)(2,1)}, u32[]{:S(2)}, u32[]{:S(2)}) %collective-permute-start) | collective-permute-done | bytes 262176 | tf_op jit(solution)/shard_map/ppermute | solution.py:372
  87.6 0.1 broadcast_in_dim.2.taps_ref
  87.7 0.0 copy-done.4
  87.7 15.6 %focus.1 = bf16[2,64,4096]{2,1,0:T(8,128)(2,1)} custom-call(bf16[2,64,32,128]{3,2,1,0:T(8,128)(2,1)S(1)} %doppler_spectra.1.body_ref, bf16[2,16,32,128]{3,2,1,0:T(8,128)(2,1)} %collective-permute-done.head_ref, bf16[2,16,32,128]{3,2,1,0:T(8,128)(2,1)S(1)} %collective-permute-done.1.tail_ref, s32[64]{0:T(128)S(1)} %dynamic_slice.6.scale_ref, ...), custom_call_target="tpu_custom_call" | custom-call | tf_op jit(solution)/shard_map/focus/pallas_call | solution.py:348
  (2 shorter events, 0.0 us)
Async XLA Ops:
  1.0 1.2 %copy-start.1 = (bf16[2,16,16384]{2,1,0:T(8,128)(2,1)S(1)}, bf16[2,16,16384]{2,1,0:T(8,128)(2,1)}, u32[]{:S(2)}) copy-start(bf16[2,16,16384]{2,1,0:T(8,128)(2,1)} %echo_ref.1) | copy-start | bytes 3145732
  2.2 1.0 %copy-start.2 = (bf16[4,256,256]{2,1,0:T(8,128)(2,1)S(1)}, bf16[4,256,256]{2,1,0:T(8,128)(2,1)}, u32[]{:S(2)}) copy-start(bf16[4,256,256]{2,1,0:T(8,128)(2,1)} %constant.28.clone.table_ref) | copy-start | bytes 1572868
  3.3 0.9 copy-start.3
  4.2 52.3 %copy-start = (bf16[32,2,128,128]{3,2,1,0:T(8,128)(2,1)S(1)}, bf16[32,2,128,128]{3,2,1,0:T(8,128)(2,1)}, u32[]{:S(2)}) copy-start(bf16[32,2,128,128]{3,2,1,0:T(8,128)(2,1)} %constant.27.clone.table_ref) | copy-start | bytes 6291460
  56.4 20.6 %copy-start.6 = (f32[8,8]{1,0:T(8,128)S(1)}, f32[8,8]{1,0:T(8,128)}, u32[]{:S(2)}) copy-start(f32[8,8]{1,0:T(8,128)} %param.15) | copy-start | bytes 772
  56.5 20.7 %copy-start.5 = (s32[4096]{0:T(1024)S(1)}, s32[4096]{0:T(1024)}, u32[]{:S(2)}) copy-start(s32[4096]{0:T(1024)} %param.14) | copy-start | bytes 49156
  56.5 31.3 %copy-start.4 = (f32[32,128]{1,0:T(8,128)S(1)}, f32[32,128]{1,0:T(8,128)}, u32[]{:S(2)}) copy-start(f32[32,128]{1,0:T(8,128)} %constant.30.clone.square_ref) | copy-start | bytes 49156
  69.3 9.9 %collective-permute-start.1 = (bf16[2,16,32,128]{3,2,1,0:T(8,128)(2,1)}, bf16[2,16,32,128]{3,2,1,0:T(8,128)(2,1)S(1)}, u32[]{:S(2)}, u32[]{:S(2)}) collective-permute-start(bf16[2,16,32,128]{3,2,1,0:T(8,128)(2,1)} %get-tuple-element.5), channel_id=1, source_target_pairs={{1,0},{2,1},{3,2},{4,3},{5,4},{6,5},{7,6},{8,7},{9,8},{10,9},{11,1... | collective-permute-start | bytes 786440 | tf_op jit(solution)/shard_map/ppermute | solution.py:373
  75.1 12.5 %collective-permute-start = (bf16[2,16,32,128]{3,2,1,0:T(8,128)(2,1)}, bf16[2,16,32,128]{3,2,1,0:T(8,128)(2,1)}, u32[]{:S(2)}, u32[]{:S(2)}) collective-permute-start(bf16[2,16,32,128]{3,2,1,0:T(8,128)(2,1)} %get-tuple-element.6), channel_id=1, source_target_pairs={{0,1},{1,2},{2,3},{3,4},{4,5},{5,6},{6,7},{7,8},{8,9},{9,10},{10,1... | collective-permute-start | bytes 786440 | tf_op jit(solution)/shard_map/ppermute | solution.py:372

commit v2 on v1

--- a/solution.py
+++ b/solution.py
@@ -78,7 +78,38 @@
     return jnp.dot(a, b, preferred_element_type=F32)
 
 
-def range_kernel(echo_ref, chirp_ref, table_ref, twiddle_ref, send_ref, wide_ref, turned_ref):
+MESH_IDS = pl.DeviceIdType.MESH
+
+
+def place():
+    wide, narrow = lax.axis_index("wide"), lax.axis_index("narrow")
+    return wide % 4, (narrow // 2) * 2 + wide // 32, (wide // 4) % 8, narrow % 2
+
+
+def device_at(x, y, z, core):
+    return ((y % 2) * 8 + z) * 4 + x, (y // 2) * 2 + core
+
+
+def signal(semaphore, x, y, z, core):
+    wide, narrow = device_at(x, y, z, core)
+    pl.semaphore_signal(
+        semaphore, inc=1, device_id={"wide": wide, "narrow": narrow}, device_id_type=MESH_IDS
+    )
+
+
+def range_kernel(
+    echo_ref, chirp_ref, table_ref, twiddle_ref, got_ref,
+    send_ref, wide_ref, turned_ref, y_sem, z_sem, send_sem, recv_sem, own_sem,
+):
+    x, y, z, core = place()
+    barrier = pltpu.get_barrier_semaphore()
+    for i in range(1, 8):
+        signal(barrier, (x + i // 2) % 4, y, z, (core + i) % 2)
+    for i in range(1, 4):
+        signal(barrier, x, (y + i) % 4, z, core)
+    for i in range(1, 8):
+        signal(barrier, x, y, (z + i) % 8, core)
+
     def spread(m, carry):
         columns = pl.ds(pl.multiple_of(m * EDGE, EDGE), EDGE)
         for part in range(2):
@@ -87,11 +118,15 @@
         return carry
 
     lax.fori_loop(0, EDGE, spread, 0, unroll=8)
+
+    pl.semaphore_wait(barrier, 17)
+    for i in range(1, 4):
+        signal(y_sem, x, (y + i) % 4, z, core)
     tc, ts = twiddle_ref[0], twiddle_ref[1]
 
     def pair(i, carry):
         b = 2 * i
-        signal = jnp.concatenate(
+        signals = jnp.concatenate(
             [
                 jnp.concatenate(
                     [wide_ref[part, pl.ds(b + h, EDGE, stride=ROWS), :] for h in range(2)], axis=1
@@ -100,7 +135,7 @@
             ],
             axis=0,
         ).astype(BF16)
-        first = dot(table_ref[0], signal)
+        first = dot(table_ref[0], signals)
         rows = []
         for h in range(2):
             re, im = first[:EDGE, h * EDGE : (h + 1) * EDGE], first[EDGE:, h * EDGE : (h + 1) * EDGE]
@@ -127,28 +162,77 @@
                 ]
         return carry
 
-    lax.fori_loop(0, ROWS // 2, pair, 0)
+    lax.fori_loop(0, ROWS // 4, pair, 0, unroll=UNROLL)
+    pl.semaphore_wait(y_sem, 3)
+    for i in range(1, 8):
+        signal(z_sem, x, y, (z + i) % 8, core)
+    lax.fori_loop(ROWS // 4, ROWS // 2, pair, 0, unroll=UNROLL)
+    pl.semaphore_wait(z_sem, 7)
+
     low_half = lax.broadcasted_iota(jnp.int32, (ROWS, EDGE), 1) < EDGE // 2
-
-    def pack(u, carry):
+    wide, narrow = device_at(x, y, z, core)
+    me = wide * 4 + narrow
+
+    def pack(t, carry):
+        z_step = jnp.where(core == 0, t % 8, (8 - t % 8) % 8)
+        x_step = (t // 8 + z_step) % 4
+        y_step = (t // 32 + z_step // 2) % 4
+        to_x, to_y, to_z = (x + x_step) % 4, (y + y_step) % 4, (z + z_step) % 8
+        to_wide, to_narrow = device_at(to_x, to_y, to_z, 0)
+        u = to_wide * 2 + to_narrow // 2
         rows = pl.ds(pl.multiple_of(u * ROWS, ROWS), ROWS)
         re, im = turned_ref[0, rows, :], turned_ref[1, rows, :]
         send_ref[2 * u] = jnp.where(low_half, re, pltpu.roll(im, EDGE // 2, 1)).astype(BF16)
         send_ref[2 * u + 1] = jnp.where(low_half, pltpu.roll(re, EDGE // 2, 1), im).astype(BF16)
-        return carry
-
-    lax.fori_loop(0, EDGE, pack, 0, unroll=8)
+
+        def start(to_core):
+            pltpu.make_async_remote_copy(
+                send_ref.at[2 * u + to_core], got_ref.at[me], send_sem, recv_sem,
+                device_id={"wide": to_wide, "narrow": to_narrow + to_core}, device_id_type=MESH_IDS,
+            ).start()
+
+        @pl.when(t > 0)
+        def _():
+            start(0)
+            start(1)
+
+        @pl.when(t == 0)
+        def _():
+            start(1 - core)
+
+        return carry
+
+    lax.fori_loop(0, EDGE, pack, 0)
+    own = pltpu.make_async_copy(send_ref.at[me], got_ref.at[me], own_sem)
+    own.start()
+    own.wait()
+    others = pltpu.make_async_remote_copy(
+        send_ref.at[pl.ds(0, DEVICES - 1)], got_ref.at[pl.ds(0, DEVICES - 1)], send_sem, recv_sem,
+        device_id={"wide": wide, "narrow": (narrow + 1) % 4}, device_id_type=MESH_IDS,
+    )
+    others.wait_send()
+    others.wait_recv()
+
+
+UNROLL = 2
 
 
 def compress(echoes, chirp, tables, twiddles):
+    semaphores = [pltpu.SemaphoreType.REGULAR] * 2 + [pltpu.SemaphoreType.DMA] * 3
     return pl.pallas_call(
         range_kernel,
         out_shape=jax.ShapeDtypeStruct((DEVICES, ROWS, EDGE), BF16),
+        in_specs=[pl.BlockSpec(memory_space=pltpu.VMEM)] * 4,
+        out_specs=pl.BlockSpec(memory_space=pltpu.VMEM),
         scratch_shapes=[
+            pltpu.VMEM((DEVICES, ROWS, EDGE), BF16),
             pltpu.VMEM((2, EDGE * ROWS, EDGE), F32),
             pltpu.VMEM((2, EDGE * ROWS, EDGE), F32),
-        ],
-        compiler_params=pltpu.CompilerParams(vmem_limit_bytes=40 << 20),
+        ]
+        + semaphores,
+        compiler_params=pltpu.CompilerParams(
+            collective_id=0, has_side_effects=True, vmem_limit_bytes=40 << 20
+        ),
         name="compress",
     )(echoes, chirp, tables, twiddles)
 
@@ -213,7 +297,7 @@
             wide_ref[part, pl.ds(k, OWN, stride=LOW), :] = result[:OWN, part * EDGE : (part + 1) * EDGE]
         return carry
 
-    lax.fori_loop(0, LOW, step, 0)
+    lax.fori_loop(0, LOW, step, 0, unroll=4)
 
     def narrow(r, carry):
         rows = pl.ds(pl.multiple_of(r * LOW, LOW), LOW)
@@ -331,7 +415,7 @@
         im_ref[k] = result[:, EDGE:]
         return carry
 
-    lax.fori_loop(0, LOW, back, 0)
+    lax.fori_loop(0, LOW, back, 0, unroll=4)
     low_transform(re_ref, im_ref, 1, low_store(re_ref, im_ref))
 
     def final(h, carry):
@@ -340,7 +424,7 @@
         image_ref[1, :, columns] = im_ref[h].astype(BF16)
         return carry
 
-    lax.fori_loop(0, LOW, final, 0)
+    lax.fori_loop(0, LOW, final, 0, unroll=4)
 
 
 def focus(body, head, tail, scales, rates, curve, square, taps, table):
@@ -366,8 +450,7 @@
     tables, twiddles = range_tables()
     azimuth = jnp.asarray(azimuth_tables())
     chirp = chirp_spectrum.reshape(2, EDGE, EDGE).transpose(0, 2, 1)
-    send = compress(echoes, chirp, jnp.asarray(tables), jnp.asarray(twiddles))
-    got = lax.all_to_all(send, AXES, 0, 0, tiled=True)
+    got = compress(echoes, chirp, jnp.asarray(tables), jnp.asarray(twiddles))
     body = doppler_spectra(got, azimuth)
     head = lax.ppermute(body[:, OWN - HALO :], AXES, [(i, i + 1) for i in range(DEVICES - 1)])
     tail = lax.ppermute(body[:, :HALO], AXES, [(i + 1, i) for i in range(DEVICES - 1)])

time: 104 us -> 81.4 us (0.78)
  blocking collectives: 44.4 us -> 0 us
  Pallas kernels: 35.6 us -> 59.4 us
  starting transfers between devices: 7.63 us -> 5.69 us
    all_to_all x1 -> x0, blocking collectives: 44.4 us -> none  [shards(): got = lax.all_to_all(send, AXES, 0, 0, tiled=True)]
    pallas_call x1, Pallas kernels: 7.87 us -> 41.2 us  [compress(): pl.pallas_call(range_kernel, out_shape=jax.ShapeDtypeStruct((DEVICES, ROW...]
    pallas_call x1, Pallas kernels: 12.1 us -> 6.07 us  [doppler_spectra(): pl.pallas_call(doppler_kernel, out_shape=jax.ShapeDtypeStruct((2, OWN, LO...]
    pallas_call x1, Pallas kernels: 15.6 us -> 12.1 us  [focus(): pl.pallas_call(focus_kernel, out_shape=jax.ShapeDtypeStruct((2, OWN, PULS...]
    ppermute x1, starting transfers between devices: 5.71 us -> 3.76 us  [shards(): lax.ppermute(body[:, :HALO], AXES, [(i + 1, i) for i in range(DEVICES - 1)])]
where the time goes in v2:
time: 81.4 us; the launch traced here: 81.1 us
  Pallas kernels  59.4 us (73%)
  waiting for transfers between devices  8.78 us (11%)
  local copies, waits for them, and re-layouts  6.3 us (8%)
  starting transfers between devices  5.69 us (7%)
    pallas_call x1, Pallas kernels, compress(): pl.pallas_call(range_kernel, out_shape=jax.ShapeDtypeStruct((DEVICES, ROW...  41.2 us
    pallas_call x1, Pallas kernels, focus(): pl.pallas_call(focus_kernel, out_shape=jax.ShapeDtypeStruct((2, OWN, PULS...  12.1 us
    ppermute x1, waiting for transfers between devices, shards(): lax.ppermute(body[:, OWN - HALO:], AXES, [(i, i + 1) for i in range(DEVIC...  8.34 us
    pallas_call x1, Pallas kernels, doppler_spectra(): pl.pallas_call(doppler_kernel, out_shape=jax.ShapeDtypeStruct((2, OWN, LO...  6.07 us
    unnamed x15, local copies, waits for them, and re-layouts  4.25 us
    ppermute x1, starting transfers between devices, shards(): lax.ppermute(body[:, :HALO], AXES, [(i + 1, i) for i in range(DEVICES - 1)])  3.76 us
    ppermute x1, starting transfers between devices, shards(): lax.ppermute(body[:, OWN - HALO:], AXES, [(i, i + 1) for i in range(DEVIC...  1.92 us
  transfers between devices with their start and end apart: 2, of which 2 were waited for; matrix products, arithmetic and copies ran while one was open for 2% of the time, Pallas kernels for 0%

profile of v2, /device:TPU:32, one launch (start us, length us, event | category | flops | bytes accessed | tf_op | source)
XLA Modules:
  0.0 81.1 jit_solution(18229784390836515401)
XLA Ops:
  0.0 0.0 copy-start
  0.0 1.1 %copy.15 = f32[1,2,128,128]{3,2,1,0:T(8,128)S(1)} copy(f32[1,2,128,128]{3,1,2,0:T(2,128)} %bitcast.9) | data formatting | bytes 262144
  1.1 0.1 copy.11
  1.2 0.0 copy-start.1
  1.2 1.2 %copy-done.1 = bf16[2,16,16384]{2,1,0:T(8,128)(2,1)S(1)} copy-done((bf16[2,16,16384]{2,1,0:T(8,128)(2,1)S(1)}, bf16[2,16,16384]{2,1,0:T(8,128)(2,1)}, u32[]{:S(2)}) %copy-start.1) | copy-done | bytes 1048600
  2.4 0.0 copy-start.2
  2.4 1.0 %copy-done.2 = bf16[4,256,256]{2,1,0:T(8,128)(2,1)S(1)} copy-done((bf16[4,256,256]{2,1,0:T(8,128)(2,1)S(1)}, bf16[4,256,256]{2,1,0:T(8,128)(2,1)}, u32[]{:S(2)}) %copy-start.2) | copy-done | bytes 524312
  3.4 0.0 copy-start.3
  3.4 0.9 %copy-done.3 = f32[2,128,128]{2,1,0:T(8,128)S(1)} copy-done((f32[2,128,128]{2,1,0:T(8,128)S(1)}, f32[2,128,128]{2,1,0:T(8,128)}, u32[]{:S(2)}) %copy-start.3) | copy-done | bytes 131096
  4.3 41.2 %compress.1.got_ref = bf16[256,16,128]{2,1,0:T(8,128)(2,1)S(1)} custom-call(bf16[2,16,16384]{2,1,0:T(8,128)(2,1)S(1)} %copy-done.1, f32[2,128,128]{2,1,0:T(8,128)S(1)} %bitcast.6, bf16[4,256,256]{2,1,0:T(8,128)(2,1)S(1)} %copy-done.2, f32[2,128,128]{2,1,0:T(8,128)S(1)} %copy-done.3), custom_call_target="tpu_custom_call" | custom-call | tf_op jit(solution)/shard_map/compress/pallas_call | solution.py:222
  45.6 0.0 copy-done
  45.6 0.0 copy-start.6
  45.6 0.0 copy-start.5
  45.6 0.0 copy-start.4
  45.6 6.1 %doppler_spectra.1.body_ref = bf16[2,64,32,128]{3,2,1,0:T(8,128)(2,1)S(1)} custom-call(bf16[256,16,128]{2,1,0:T(8,128)(2,1)S(1)} %compress.1.got_ref, bf16[32,2,128,128]{3,2,1,0:T(8,128)(2,1)S(1)} %copy-done), custom_call_target="tpu_custom_call" | custom-call | tf_op jit(solution)/shard_map/doppler_spectra/pallas_call | solution.py:312
  51.7 0.8 %fusion = (bf16[2,16,32,128]{3,2,1,0:T(8,128)(2,1)}, bf16[2,16,32,128]{3,2,1,0:T(8,128)(2,1)}) fusion(bf16[2,64,32,128]{3,2,1,0:T(8,128)(2,1)S(1)} %doppler_spectra.1.body_ref), kind=kLoop, calls=%fused_computation.2 | loop fusion | bytes 1048576 | tf_op jit(solution)/shard_map/slice | solution.py:456
  52.5 3.8 %collective-permute-start.1 = (bf16[2,16,32,128]{3,2,1,0:T(8,128)(2,1)}, bf16[2,16,32,128]{3,2,1,0:T(8,128)(2,1)S(1)}, u32[]{:S(2)}, u32[]{:S(2)}) collective-permute-start(bf16[2,16,32,128]{3,2,1,0:T(8,128)(2,1)} %get-tuple-element.5), channel_id=1, source_target_pairs={{1,0},{2,1},{3,2},{4,3},{5,4},{6,5},{7,6},{8,7},{9,8},{10,9},{11,1... | collective-permute-start | bytes 786440 | tf_op jit(solution)/shard_map/ppermute | solution.py:456
  56.3 1.9 %collective-permute-start = (bf16[2,16,32,128]{3,2,1,0:T(8,128)(2,1)}, bf16[2,16,32,128]{3,2,1,0:T(8,128)(2,1)}, u32[]{:S(2)}, u32[]{:S(2)}) collective-permute-start(bf16[2,16,32,128]{3,2,1,0:T(8,128)(2,1)} %get-tuple-element.6), channel_id=1, source_target_pairs={{0,1},{1,2},{2,3},{3,4},{4,5},{5,6},{6,7},{7,8},{8,9},{9,10},{10,1... | collective-permute-start | bytes 786440 | tf_op jit(solution)/shard_map/ppermute | solution.py:455
  58.2 0.0 copy-done.6
  58.2 0.1 convert_element_type.16
  58.3 0.0 copy-done.5
  58.3 0.1 reshape.16
  58.4 0.1 copy.12
  58.5 0.8 dynamic_slice.6.scale_ref
  59.3 0.8 dynamic-slice_multiply_fusion.rate_ref
  60.0 0.4 collective-permute-done.1.tail_ref
  60.5 8.3 %collective-permute-done.head_ref = bf16[2,16,32,128]{3,2,1,0:T(8,128)(2,1)} collective-permute-done((bf16[2,16,32,128]{3,2,1,0:T(8,128)(2,1)}, bf16[2,16,32,128]{3,2,1,0:T(8,128)(2,1)}, u32[]{:S(2)}, u32[]{:S(2)}) %collective-permute-start) | collective-permute-done | bytes 262176 | tf_op jit(solution)/shard_map/ppermute | solution.py:455
  68.8 0.1 broadcast_in_dim.2.taps_ref
  68.9 0.0 copy-done.4
  69.0 12.1 %focus.1 = bf16[2,64,4096]{2,1,0:T(8,128)(2,1)} custom-call(bf16[2,64,32,128]{3,2,1,0:T(8,128)(2,1)S(1)} %doppler_spectra.1.body_ref, bf16[2,16,32,128]{3,2,1,0:T(8,128)(2,1)} %collective-permute-done.head_ref, bf16[2,16,32,128]{3,2,1,0:T(8,128)(2,1)S(1)} %collective-permute-done.1.tail_ref, s32[64]{0:T(128)S(1)} %dynamic_slice.6.scale_ref, ...), custom_call_target="tpu_custom_call" | custom-call | tf_op jit(solution)/shard_map/focus/pallas_call | solution.py:432
  (2 shorter events, 0.0 us)
Async XLA Ops:
  0.0 45.6 %copy-start = (bf16[32,2,128,128]{3,2,1,0:T(8,128)(2,1)S(1)}, bf16[32,2,128,128]{3,2,1,0:T(8,128)(2,1)}, u32[]{:S(2)}) copy-start(bf16[32,2,128,128]{3,2,1,0:T(8,128)(2,1)} %constant.27.clone.table_ref) | copy-start | bytes 6291460
  1.2 1.2 %copy-start.1 = (bf16[2,16,16384]{2,1,0:T(8,128)(2,1)S(1)}, bf16[2,16,16384]{2,1,0:T(8,128)(2,1)}, u32[]{:S(2)}) copy-start(bf16[2,16,16384]{2,1,0:T(8,128)(2,1)} %echo_ref.1) | copy-start | bytes 3145732
  2.4 1.0 %copy-start.2 = (bf16[4,256,256]{2,1,0:T(8,128)(2,1)S(1)}, bf16[4,256,256]{2,1,0:T(8,128)(2,1)}, u32[]{:S(2)}) copy-start(bf16[4,256,256]{2,1,0:T(8,128)(2,1)} %constant.28.clone.table_ref) | copy-start | bytes 1572868
  3.4 0.9 %copy-start.3 = (f32[2,128,128]{2,1,0:T(8,128)S(1)}, f32[2,128,128]{2,1,0:T(8,128)}, u32[]{:S(2)}) copy-start(f32[2,128,128]{2,1,0:T(8,128)} %constant.29.clone.twiddle_ref) | copy-start | bytes 393220
  45.6 12.7 %copy-start.6 = (f32[8,8]{1,0:T(8,128)S(1)}, f32[8,8]{1,0:T(8,128)}, u32[]{:S(2)}) copy-start(f32[8,8]{1,0:T(8,128)} %param.15) | copy-start | bytes 772
  45.6 12.7 %copy-start.5 = (s32[4096]{0:T(1024)S(1)}, s32[4096]{0:T(1024)}, u32[]{:S(2)}) copy-start(s32[4096]{0:T(1024)} %param.14) | copy-start | bytes 49156
  45.6 23.4 %copy-start.4 = (f32[32,128]{1,0:T(8,128)S(1)}, f32[32,128]{1,0:T(8,128)}, u32[]{:S(2)}) copy-start(f32[32,128]{1,0:T(8,128)} %constant.30.clone.square_ref) | copy-start | bytes 49156
  52.5 8.0 %collective-permute-start.1 = (bf16[2,16,32,128]{3,2,1,0:T(8,128)(2,1)}, bf16[2,16,32,128]{3,2,1,0:T(8,128)(2,1)S(1)}, u32[]{:S(2)}, u32[]{:S(2)}) collective-permute-start(bf16[2,16,32,128]{3,2,1,0:T(8,128)(2,1)} %get-tuple-element.5), channel_id=1, source_target_pairs={{1,0},{2,1},{3,2},{4,3},{5,4},{6,5},{7,6},{8,7},{9,8},{10,9},{11,1... | collective-permute-start | bytes 786440 | tf_op jit(solution)/shard_map/ppermute | solution.py:456
  56.3 12.5 %collective-permute-start = (bf16[2,16,32,128]{3,2,1,0:T(8,128)(2,1)}, bf16[2,16,32,128]{3,2,1,0:T(8,128)(2,1)}, u32[]{:S(2)}, u32[]{:S(2)}) collective-permute-start(bf16[2,16,32,128]{3,2,1,0:T(8,128)(2,1)} %get-tuple-element.6), channel_id=1, source_target_pairs={{0,1},{1,2},{2,3},{3,4},{4,5},{5,6},{6,7},{7,8},{8,9},{9,10},{10,1... | collective-permute-start | bytes 786440 | tf_op jit(solution)/shard_map/ppermute | solution.py:455

commit v3 on v2

v3 whole, which is shorter than its diff:
```python
import functools
import math

import jax
import jax.numpy as jnp
import ml_dtypes
import numpy as np
from jax import lax
from jax.experimental import pallas as pl
from jax.experimental.pallas import tpu as pltpu
from jax.sharding import PartitionSpec as P

PULSES = 4096
BINS = 16384
EDGE = 128
LOW = 32
TAPS = 8
PHASES = 8
HALO = 16
DEVICES = 256
OWN = BINS // DEVICES
ROWS = PULSES // DEVICES
AXES = ("wide", "narrow")
F32 = jnp.float32
BF16 = jnp.bfloat16


def roots(product, total):
    angles = 2.0 * np.pi / total * (product % total)
    return np.cos(angles), np.sin(angles)


def range_tables():
    count = np.arange(EDGE)
    c, s = roots(np.outer(count, count), EDGE)
    c, s = c / math.sqrt(EDGE), s / math.sqrt(EDGE)
    fwd_left = np.block([[c, s], [-s, c]])
    inv_left = np.block([[c, -s], [s, c]])
    tables = np.stack([fwd_left, fwd_left.T, inv_left.T, inv_left])
    tc, ts = roots(np.outer(count, count), BINS)
    return tables.astype(ml_dtypes.bfloat16), np.stack([tc, ts]).astype(np.float32)


def azimuth_tables():
    low = np.arange(LOW)[:, None, None]
    n = np.arange(EDGE)[None, :, None]
    j = np.arange(EDGE)[None, None, :]
    c, s = roots(n * (low + LOW * j), PULSES)
    return (np.stack([c, s], axis=1) / math.sqrt(PULSES)).astype(ml_dtypes.bfloat16)


def fft(values, sign):
    count = len(values)
    if count == 1:
        return values
    even, odd = fft(values[0::2], sign), fft(values[1::2], sign)
    half = count // 2
    out = [None] * count
    for k in range(half):
        (ar, ai), (br, bi) = even[k], odd[k]
        if k == 0:
            tr, ti = br, bi
        elif 4 * k == count:
            tr, ti = (-bi, br) if sign > 0 else (bi, -br)
        else:
            angle = 2.0 * math.pi * k / count
            c, s = math.cos(angle), sign * math.sin(angle)
            if 8 * k == count:
                tr, ti = (br - bi * (1 if sign > 0 else -1)) * c, (bi + br * (1 if sign > 0 else -1)) * c
            else:
                tr, ti = br * c - bi * s, br * s + bi * c
        out[k] = (ar + tr, ai + ti)
        out[k + half] = (ar - tr, ai - ti)
    return out


def dot(a, b):
    return jnp.dot(a, b, preferred_element_type=F32)


MESH_IDS = pl.DeviceIdType.MESH


def place():
    wide, narrow = lax.axis_index("wide"), lax.axis_index("narrow")
    return wide % 4, (narrow // 2) * 2 + wide // 32, (wide // 4) % 8, narrow % 2


def device_at(x, y, z, core):
    return ((y % 2) * 8 + z) * 4 + x, (y // 2) * 2 + core


def signal(semaphore, x, y, z, core):
    wide, narrow = device_at(x, y, z, core)
    pl.semaphore_signal(
        semaphore, inc=1, device_id={"wide": wide, "narrow": narrow}, device_id_type=MESH_IDS
    )


def split_pairs(got_ref, re_ref, im_ref):
    half = EDGE // 2
    low_half = lax.broadcasted_iota(jnp.int32, (ROWS, EDGE), 1) < half

    def step(m, carry):
        for g in range(half // ROWS):
            near = got_ref[m * 8 + g].astype(F32)
            far = got_ref[m * 8 + 4 + g].astype(F32)
            rows = pl.ds(g * ROWS, ROWS)
            re_ref[m, rows, :] = jnp.where(low_half, near, pltpu.roll(far, half, 1))
            im_ref[m, rows, :] = jnp.where(low_half, pltpu.roll(near, half, 1), far)
        return carry

    lax.fori_loop(0, LOW, step, 0, unroll=2)


def low_transform(re_ref, im_ref, sign, block, store):
    def step(g, carry):
        rows = pl.ds(pl.multiple_of(g * block, block), block)
        values = fft([(re_ref[m, rows, :], im_ref[m, rows, :]) for m in range(LOW)], sign)
        for k, (re, im) in enumerate(values):
            store(k, rows, re, im)
        return carry

    lax.fori_loop(0, EDGE // 2 // block, step, 0)


def low_store(re_ref, im_ref):
    def store(k, rows, re, im):
        re_ref[k, rows, :] = re
        im_ref[k, rows, :] = im

    return store


def block_table(table_ref, k):
    c, s = table_ref[k, 0], table_ref[k, 1]
    return jnp.concatenate(
        [jnp.concatenate([c, -s], axis=1), jnp.concatenate([s, c], axis=1)], axis=0
    )


def turn(turns):
    x = turns - jnp.round(turns)
    y = x * x
    c = jnp.full_like(x, COS_TERMS[-1])
    for term in COS_TERMS[-2::-1]:
        c = c * y + term
    s = jnp.full_like(x, SIN_TERMS[-1])
    for term in SIN_TERMS[-2::-1]:
        s = s * y + term
    return c, s * x


def fitted_terms():
    x = np.cos(np.pi * (np.arange(400) + 0.5) / 800) * 0.5
    y = x * x
    powers = np.stack([y**i for i in range(6)], axis=1)
    c = np.linalg.lstsq(powers, np.cos(2 * np.pi * x), rcond=None)[0]
    s = np.linalg.lstsq(powers * x[:, None], np.sin(2 * np.pi * x), rcond=None)[0]
    return [float(v) for v in c], [float(v) for v in s]


COS_TERMS, SIN_TERMS = fitted_terms()


def order_curve(angle_ref, curve_ref):
    values = angle_ref[...].astype(F32)
    upper = jnp.floor(values * (1.0 / 64.0))
    lower = values - 64.0 * upper
    row = lax.broadcasted_iota(jnp.int32, (LOW, EDGE), 0)
    lane = lax.broadcasted_iota(jnp.int32, (LOW, EDGE), 1)
    total = jnp.zeros((LOW, EDGE), F32)
    for digit, size in ((upper, 64.0), (lower, 1.0)):
        digit = digit.astype(BF16)
        for i in range(EDGE // LOW):
            pick = jnp.where(lane == LOW * i + row, 1.0, 0.0).astype(BF16)
            part = lax.dot_general(pick, digit, (((1,), (1,)), ((), ())), preferred_element_type=F32)
            place_at = jnp.where(lane == 4 * row + i, 1.0, 0.0).astype(BF16)
            total = total + size * dot(part.astype(BF16), place_at)
    curve_ref[...] = total


def prepare_rows(r, scale, rate, curve_ref, square_ref, taps_ref, bit_ref, weight_ref, phase_ref):
    offset = jnp.where(scale < 0, 8.0 * SHIFT_LOW, 0.0).astype(F32)
    scale = scale.astype(F32) * (1.0 / 4096.0)
    for h in range(2):
        rows = pl.ds(16 * h, 16)
        level = (jnp.floor(curve_ref[rows, :] * scale) + offset).astype(BF16)
        bits = []
        for i, weight in enumerate((64, 32, 16, 8, 4, 2, 1)):
            bit = level >= jnp.asarray(weight, BF16)
            bits.append(bit)
            if i < 4:
                bit_ref[r, i, rows, :] = jnp.where(bit, jnp.asarray(1, BF16), jnp.asarray(0, BF16))
            if weight > 1:
                level = jnp.where(bit, level - jnp.asarray(weight, BF16), level)
        for t in range(TAPS):
            level4 = [jnp.where(bits[6], taps_ref[(2 * i + 1) * TAPS + t], taps_ref[2 * i * TAPS + t]) for i in range(4)]
            level2 = [jnp.where(bits[5], level4[2 * i + 1], level4[2 * i]) for i in range(2)]
            weight_ref[r, t, rows, :] = jnp.where(bits[4], level2[1], level2[0])
        c, s = turn(square_ref[rows, :] * rate)
        phase_ref[0, r, rows, :] = c
        phase_ref[1, r, rows, :] = s


def migrate_rows(r, scale, padded_ref, bit_ref, weight_ref, phase_ref, store):
    first = r + HALO - 3 - jnp.where(scale < 0, SHIFT_LOW, 0)
    for h in range(2):
        rows = pl.ds(16 * h, 16)
        bits = [bit_ref[r, i, rows, :] > jnp.asarray(0, BF16) for i in range(4)]
        sums = []
        for part in range(2):
            x = [padded_ref[part, first + i, rows, :] for i in range(21)]
            x = [jnp.where(bits[0], x[i + 8], x[i]) if i < 13 else x[i] for i in range(15)]
            x = [jnp.where(bits[1], x[i + 4], x[i]) for i in range(11)]
            x = [jnp.where(bits[2], x[i + 2], x[i]) for i in range(9)]
            x = [jnp.where(bits[3], x[i + 1], x[i]) for i in range(8)]
            terms = [x[t] * weight_ref[r, t, rows, :] for t in range(TAPS)]
            while len(terms) > 1:
                terms = [terms[i] + terms[i + 1] for i in range(0, len(terms), 2)]
            sums.append(terms[0].astype(F32))
        c, s = phase_ref[0, r, rows, :], phase_ref[1, r, rows, :]
        store(r, h, sums[0] * c - sums[1] * s, sums[0] * s + sums[1] * c)


SHIFT_LOW = 13


def main_kernel(
    echo_hbm, chirp_hbm, table_hbm, twiddle_hbm, azimuth_hbm, scale_hbm, rate_hbm, angle_hbm, square_hbm, kernel_hbm,
    image_ref,
    echo_ref, line_ref, table_ref, twiddle_ref, azimuth_ref, scale_ref, rate_ref, angle_ref, square_ref, kernel_ref,
    chirp_ref, curve_ref, taps_ref, bit_ref, weight_ref, phase_ref,
    send_ref, got_ref, wide_ref, turned_ref, re_ref, im_ref, padded_ref, head_ref, tail_ref,
    load_sems, y_sem, z_sem, send_sem, recv_sem, own_sem, halo_send, halo_recv,
):
    x, y, z, core = place()
    wide, narrow = device_at(x, y, z, core)
    me = wide * 4 + narrow

    pieces = 4
    echo_loads = []
    for i in range(pieces):
        columns = pl.ds(i * (BINS // pieces), BINS // pieces)
        load = pltpu.make_async_copy(
            echo_hbm.at[:, :, columns], echo_ref.at[:, :, columns], load_sems.at[i]
        )
        load.start()
        echo_loads.append(load)
    own_rows = pl.ds(pl.multiple_of(me // 16 * 8, 8), 8)
    loads = []
    for i, (source, target) in enumerate(
        (
            (chirp_hbm, line_ref), (table_hbm, table_ref), (twiddle_hbm, twiddle_ref),
            (azimuth_hbm, azimuth_ref), (angle_hbm, angle_ref), (square_hbm, square_ref), (kernel_hbm, kernel_ref),
            (scale_hbm.at[own_rows], scale_ref), (rate_hbm.at[own_rows], rate_ref),
        )
    ):
        load = pltpu.make_async_copy(source, target, load_sems.at[pieces + i])
        load.start()
        loads.append(load)

    barrier = pltpu.get_barrier_semaphore()
    for i in range(1, 8):
        signal(barrier, (x + i // 2) % 4, y, z, (core + i) % 2)
    for i in range(1, 4):
        signal(barrier, x, (y + i) % 4, z, core)
    for i in range(1, 8):
        signal(barrier, x, y, (z + i) % 8, core)

    def spread(m, carry):
        columns = pl.ds(pl.multiple_of(m * EDGE, EDGE), EDGE)
        for part in range(2):
            block = echo_ref[part, :, columns].astype(F32)
            wide_ref[part, pl.ds(pl.multiple_of(m * ROWS, ROWS), ROWS), :] = block
        return carry

    for i in range(pieces):
        echo_loads[i].wait()
        lax.fori_loop(i * (EDGE // pieces), (i + 1) * (EDGE // pieces), spread, 0, unroll=8)
    for load in loads[:3]:
        load.wait()

    def lay(j, carry):
        for part in range(2):
            chirp_ref[part, pl.ds(j, 1), :] = line_ref[part : part + 1, pl.ds(pl.multiple_of(j * EDGE, EDGE), EDGE)]
        return carry

    lax.fori_loop(0, EDGE, lay, 0, unroll=8)
    for part in range(2):
        chirp_ref[part] = chirp_ref[part].T

    pl.semaphore_wait(barrier, 17)
    for i in range(1, 4):
        signal(y_sem, x, (y + i) % 4, z, core)
    tc, ts = twiddle_ref[0], twiddle_ref[1]

    def pair(i, carry):
        b = 2 * i
        signals = jnp.concatenate(
            [
                jnp.concatenate(
                    [wide_ref[part, pl.ds(b + h, EDGE, stride=ROWS), :] for h in range(2)], axis=1
                )
                for part in range(2)
            ],
            axis=0,
        ).astype(BF16)
        first = dot(table_ref[0], signals)
        rows = []
        for h in range(2):
            re, im = first[:EDGE, h * EDGE : (h + 1) * EDGE], first[EDGE:, h * EDGE : (h + 1) * EDGE]
            rows.append(jnp.concatenate([re * tc + im * ts, im * tc - re * ts], axis=1))
        spectrum = dot(jnp.concatenate(rows, axis=0).astype(BF16), table_ref[1])
        rows = []
        for h in range(2):
            re, im = spectrum[h * EDGE : (h + 1) * EDGE, :EDGE], spectrum[h * EDGE : (h + 1) * EDGE, EDGE:]
            rows.append(
                jnp.concatenate(
                    [re * chirp_ref[0] - im * chirp_ref[1], re * chirp_ref[1] + im * chirp_ref[0]], axis=1
                )
            )
        back = dot(jnp.concatenate(rows, axis=0).astype(BF16), table_ref[2])
        columns = []
        for h in range(2):
            re, im = back[h * EDGE : (h + 1) * EDGE, :EDGE], back[h * EDGE : (h + 1) * EDGE, EDGE:]
            columns.append(jnp.concatenate([re * tc - im * ts, im * tc + re * ts], axis=0))
        result = dot(table_ref[3], jnp.concatenate(columns, axis=1).astype(BF16))
        for h in range(2):
            for part in range(2):
                turned_ref[part, pl.ds(b + h, EDGE, stride=ROWS), :] = result[
                    part * EDGE : (part + 1) * EDGE, h * EDGE : (h + 1) * EDGE
                ]
        return carry

    lax.fori_loop(0, ROWS // 4, pair, 0, unroll=UNROLL)
    pl.semaphore_wait(y_sem, 3)
    for i in range(1, 8):
        signal(z_sem, x, y, (z + i) % 8, core)
    lax.fori_loop(ROWS // 4, ROWS // 2, pair, 0, unroll=UNROLL)
    low_half = lax.broadcasted_iota(jnp.int32, (ROWS, EDGE), 1) < EDGE // 2

    def pack(u, carry):
        rows = pl.ds(pl.multiple_of(u * ROWS, ROWS), ROWS)
        re, im = turned_ref[0, rows, :], turned_ref[1, rows, :]
        send_ref[2 * u] = jnp.where(low_half, re, pltpu.roll(im, EDGE // 2, 1)).astype(BF16)
        send_ref[2 * u + 1] = jnp.where(low_half, pltpu.roll(re, EDGE // 2, 1), im).astype(BF16)
        return carry

    lax.fori_loop(0, EDGE, pack, 0, unroll=8)
    pl.semaphore_wait(z_sem, 7)

    def start(to_wide, to_narrow, to):
        pltpu.make_async_remote_copy(
            send_ref.at[to], got_ref.at[me], send_sem, recv_sem,
            device_id={"wide": to_wide, "narrow": to_narrow}, device_id_type=MESH_IDS,
        ).start()

    def spread_out(t, carry):
        z_step = jnp.where(core == 0, t % 8, (8 - t % 8) % 8)
        x_step = (t // 8 + z_step) % 4
        y_step = (t // 32 + z_step // 2) % 4
        to_wide, to_narrow = device_at((x + x_step) % 4, (y + y_step) % 4, (z + z_step) % 8, 0)
        to = to_wide * 4 + to_narrow
        start(to_wide, to_narrow, to)
        start(to_wide, to_narrow + 1, to + 1)
        return carry

    start(wide, narrow + 1 - 2 * core, me + 1 - 2 * core)
    lax.fori_loop(1, EDGE, spread_out, 0)
    own = pltpu.make_async_copy(send_ref.at[me], got_ref.at[me], own_sem)
    own.start()
    own.wait()

    for load in loads[3:]:
        load.wait()
    order_curve(angle_ref, curve_ref)
    for i in range(PHASES * TAPS):
        tap = kernel_ref[i // TAPS : i // TAPS + 1, i % TAPS : i % TAPS + 1]
        taps_ref[i] = jnp.broadcast_to(tap, (16, EDGE)).astype(BF16)
    scale_row, scale_column = me // 2 % 8, me % 2 * OWN

    def prepare(r, carry):
        prepare_rows(
            r, scale_ref[scale_row, scale_column + r], rate_ref[scale_row, scale_column + r] * 0.5,
            curve_ref, square_ref, taps_ref, bit_ref, weight_ref, phase_ref,
        )
        return carry

    lax.fori_loop(0, OWN, prepare, 0)
    others = pltpu.make_async_remote_copy(
        send_ref.at[pl.ds(0, DEVICES - 1)], got_ref.at[pl.ds(0, DEVICES - 1)], send_sem, recv_sem,
        device_id={"wide": wide, "narrow": (narrow + 1) % 4}, device_id_type=MESH_IDS,
    )
    others.wait_send()
    others.wait_recv()


    half = EDGE // 2
    split_pairs(got_ref, re_ref, im_ref)
    low_transform(re_ref, im_ref, -1, 8, low_store(re_ref, im_ref))

    def high(k, carry):
        re, im = re_ref[k], im_ref[k]
        left = jnp.concatenate(
            [re, pltpu.roll(re, half, 1), im, pltpu.roll(im, half, 1)], axis=0
        ).astype(BF16)
        result = lax.dot_general(
            left, block_table(azimuth_ref, k), (((0,), (0,)), ((), ())), preferred_element_type=F32
        )
        for part in range(2):
            wide_ref[part, pl.ds(k, OWN, stride=LOW), :] = result[:OWN, part * EDGE : (part + 1) * EDGE]
        return carry

    halos = []
    for h in range(2):
        lax.fori_loop(16 * h, 16 * h + 16, high, 0, unroll=4)

        def narrowed(r, carry, h=h):
            rows = pl.ds(pl.multiple_of(r * LOW + 16 * h, 16), 16)
            for part in range(2):
                padded_ref[part, HALO + r, 16 * h : 16 * h + 16, :] = wide_ref[part, rows, :].astype(BF16)
            return carry

        lax.fori_loop(0, OWN, narrowed, 0, unroll=8)
        k_rows = pl.ds(16 * h, 16)
        for side in range(2):
            other = (me + 1 - 2 * side + DEVICES) % DEVICES
            first = OWN if side == 0 else HALO
            target = head_ref if side == 0 else tail_ref
            halo = pltpu.make_async_remote_copy(
                padded_ref.at[:, pl.ds(first, HALO), k_rows, :], target.at[:, :, k_rows, :],
                halo_send.at[2 * h + side], halo_recv.at[2 * h + side],
                device_id={"wide": other // 4, "narrow": other % 4}, device_id_type=MESH_IDS,
            )
            halo.start()
            halos.append(halo)

    def store(r, h, re, im):
        rows = pl.ds(pl.multiple_of(r * LOW + 16 * h, 16), 16)
        turned_ref[0, rows, :] = re
        turned_ref[1, rows, :] = im

    def migrate(r):
        migrate_rows(
            r, scale_ref[scale_row, scale_column + r], padded_ref, bit_ref, weight_ref, phase_ref, store
        )

    def inner(r, carry):
        migrate(r)
        return carry

    lax.fori_loop(HALO, OWN - HALO, inner, 0)
    for halo in halos:
        halo.wait()

    def edge(r, carry):
        for part in range(2):
            padded_ref[part, r] = jnp.where(me == 0, jnp.zeros((LOW, EDGE), BF16), head_ref[part, r])
            padded_ref[part, HALO + OWN + r] = jnp.where(
                me == DEVICES - 1, jnp.zeros((LOW, EDGE), BF16), tail_ref[part, r]
            )
        return carry

    lax.fori_loop(0, HALO, edge, 0)

    def outer(i, carry):
        migrate(jnp.where(i < HALO, i, i + OWN - 2 * HALO))
        return carry

    lax.fori_loop(0, 2 * HALO, outer, 0)

    def back(k, carry):
        left = jnp.concatenate(
            [turned_ref[part, pl.ds(k, OWN, stride=LOW), :] for part in range(2)], axis=1
        ).astype(BF16)
        result = lax.dot_general(
            left, block_table(azimuth_ref, k), (((1,), (1,)), ((), ())), preferred_element_type=F32
        )
        re_ref[k] = result[:, :EDGE]
        im_ref[k] = result[:, EDGE:]
        return carry

    lax.fori_loop(0, LOW, back, 0, unroll=4)

    def finish(h, rows, re, im):
        image_ref[0, rows, h * EDGE : (h + 1) * EDGE] = re.astype(BF16)
        image_ref[1, rows, h * EDGE : (h + 1) * EDGE] = im.astype(BF16)

    low_transform(re_ref, im_ref, 1, 16, finish)


UNROLL = 2
VMEM_BYTES = 63 << 20


def focused_image(*operands):
    big = pltpu.VMEM((2, EDGE * ROWS, EDGE), F32)
    scratch = [pltpu.VMEM(operand.shape, operand.dtype) for operand in operands[:5]]
    scratch += [pltpu.SMEM((8, EDGE), jnp.int32), pltpu.SMEM((8, EDGE), F32)]
    scratch += [pltpu.VMEM(operand.shape, operand.dtype) for operand in operands[7:]]
    scratch += [
        pltpu.VMEM((2, EDGE, EDGE), F32),
        pltpu.VMEM((LOW, EDGE), F32),
        pltpu.VMEM((PHASES * TAPS, 16, EDGE), BF16),
        pltpu.VMEM((OWN, 4, LOW, EDGE), BF16),
        pltpu.VMEM((OWN, TAPS, LOW, EDGE), BF16),
        pltpu.VMEM((2, OWN, LOW, EDGE), F32),
        pltpu.VMEM((DEVICES, ROWS, EDGE), BF16),
        pltpu.VMEM((DEVICES, ROWS, EDGE), BF16),
        big,
        big,
        pltpu.VMEM((LOW, EDGE // 2, EDGE), F32),
        pltpu.VMEM((LOW, EDGE // 2, EDGE), F32),
        pltpu.VMEM((2, 2 * HALO + OWN + 8, LOW, EDGE), BF16),
        pltpu.VMEM((2, HALO, LOW, EDGE), BF16),
        pltpu.VMEM((2, HALO, LOW, EDGE), BF16),
        pltpu.SemaphoreType.DMA((13,)),
        pltpu.SemaphoreType.REGULAR,
        pltpu.SemaphoreType.REGULAR,
        pltpu.SemaphoreType.DMA,
        pltpu.SemaphoreType.DMA,
        pltpu.SemaphoreType.DMA,
        pltpu.SemaphoreType.DMA((4,)),
        pltpu.SemaphoreType.DMA((4,)),
    ]
    return pl.pallas_call(
        main_kernel,
        out_shape=jax.ShapeDtypeStruct((2, OWN, PULSES), BF16),
        in_specs=[pl.BlockSpec(memory_space=pl.ANY)] * 10,
        out_specs=pl.BlockSpec(memory_space=pltpu.VMEM),
        scratch_shapes=scratch,
        compiler_params=pltpu.CompilerParams(
            collective_id=0, has_side_effects=True, vmem_limit_bytes=VMEM_BYTES
        ),
        name="focused_image",
    )(*operands)


def shards(echoes, chirp_spectrum, fm_rate, range_scale, doppler_curve, kernels):
    tables, twiddles = range_tables()
    index = np.arange(PULSES)
    signed = (index + PULSES // 2) % PULSES - PULSES // 2
    square = np.ascontiguousarray((signed * signed).astype(np.float32).reshape(EDGE, LOW).T)
    return focused_image(
        echoes, chirp_spectrum, jnp.asarray(tables), jnp.asarray(twiddles), jnp.asarray(azimuth_tables()),
        range_scale.reshape(EDGE, EDGE), fm_rate.reshape(EDGE, EDGE),
        doppler_curve.reshape(LOW, EDGE), jnp.asarray(square), kernels,
    )


def solution(mesh):
    in_specs = (P(None, AXES, None), P(), P(), P(), P(), P())
    out_specs = P(None, AXES, None)
    return jax.shard_map(shards, mesh=mesh, in_specs=in_specs, out_specs=out_specs, check_vma=False)
```

time: 81.4 us -> 64.5 us (0.79)
  the two profiles are of different devices: /device:TPU:32 before, /device:TPU:1 now
where the time goes in v3:
time: 64.5 us; the launch traced here: 64.4 us
  Pallas kernels  62.1 us (96%)
  local copies, waits for them, and re-layouts  2.29 us (4%)
    pallas_call x1, Pallas kernels, focused_image(): pl.pallas_call(main_kernel, out_shape=jax.ShapeDtypeStruct((2, OWN, PULSE...  62.1 us
    unnamed x1, local copies, waits for them, and re-layouts  2.29 us

profile of v3, /device:TPU:1, one launch (start us, length us, event | category | flops | bytes accessed | tf_op | source)
XLA Modules:
  0.0 64.4 jit_solution(1629062943267392154)
XLA Ops:
  0.0 62.1 %focused_image.1 = bf16[2,64,4096]{2,1,0:T(8,128)(2,1)} custom-call(bf16[2,16,16384]{2,1,0:T(8,128)(2,1)} %echo_hbm.1, f32[2,16384]{1,0:T(2,128)} %chirp_hbm.1, bf16[4,256,256]{2,1,0:T(8,128)(2,1)} %constant.8.clone.table_hbm, f32[2,128,128]{2,1,0:T(8,128)} %constant.9.clone.twiddle_hbm, bf16[32,2,128,128]{3,2,1,0:T(8,128)(2,1)} %constant.10.clone.azimuth_hbm, ...), custom_call_target="tpu_custom_call" | custom-call | tf_op jit(solution)/shard_map/focused_image/pallas_call | solution.py:527
  62.1 2.3 %copy.12 = bf16[2,64,4096]{2,1,0:T(8,128)(2,1)} copy(bf16[2,64,4096]{2,1,0:T(8,128)(2,1)} %focused_image.1) | data formatting | bytes 2097152

commit v4 on v3

--- a/solution.py
+++ b/solution.py
@@ -46,7 +46,11 @@
     n = np.arange(EDGE)[None, :, None]
     j = np.arange(EDGE)[None, None, :]
     c, s = roots(n * (low + LOW * j), PULSES)
-    return (np.stack([c, s], axis=1) / math.sqrt(PULSES)).astype(ml_dtypes.bfloat16)
+    forward = np.concatenate(
+        [np.concatenate([c, -s], axis=2), np.concatenate([s, c], axis=2)], axis=1
+    ) / math.sqrt(PULSES)
+    inverse = np.ascontiguousarray(forward.transpose(0, 2, 1))
+    return forward.astype(ml_dtypes.bfloat16), inverse.astype(ml_dtypes.bfloat16)
 
 
 def fft(values, sign):
@@ -113,15 +117,15 @@
     lax.fori_loop(0, LOW, step, 0, unroll=2)
 
 
-def low_transform(re_ref, im_ref, sign, block, store):
+def low_transform(re_ref, im_ref, sign, block, store, first=0, count=8, stride=8):
     def step(g, carry):
-        rows = pl.ds(pl.multiple_of(g * block, block), block)
+        rows = pl.ds(pl.multiple_of(first + g * stride, block), block)
         values = fft([(re_ref[m, rows, :], im_ref[m, rows, :]) for m in range(LOW)], sign)
         for k, (re, im) in enumerate(values):
             store(k, rows, re, im)
         return carry
 
-    lax.fori_loop(0, EDGE // 2 // block, step, 0)
+    lax.fori_loop(0, count, step, 0)
 
 
 def low_store(re_ref, im_ref):
@@ -130,13 +134,6 @@
         im_ref[k, rows, :] = im
 
     return store
-
-
-def block_table(table_ref, k):
-    c, s = table_ref[k, 0], table_ref[k, 1]
-    return jnp.concatenate(
-        [jnp.concatenate([c, -s], axis=1), jnp.concatenate([s, c], axis=1)], axis=0
-    )
 
 
 def turn(turns):
@@ -203,9 +200,9 @@
         phase_ref[1, r, rows, :] = s
 
 
-def migrate_rows(r, scale, padded_ref, bit_ref, weight_ref, phase_ref, store):
+def migrate_rows(r, scale, halves, padded_ref, bit_ref, weight_ref, phase_ref, store):
     first = r + HALO - 3 - jnp.where(scale < 0, SHIFT_LOW, 0)
-    for h in range(2):
+    for h in halves:
         rows = pl.ds(16 * h, 16)
         bits = [bit_ref[r, i, rows, :] > jnp.asarray(0, BF16) for i in range(4)]
         sums = []
@@ -227,12 +224,13 @@
 
 
 def main_kernel(
-    echo_hbm, chirp_hbm, table_hbm, twiddle_hbm, azimuth_hbm, scale_hbm, rate_hbm, angle_hbm, square_hbm, kernel_hbm,
+    echo_hbm, chirp_hbm, table_hbm, twiddle_hbm, azimuth_hbm, scale_hbm, rate_hbm, angle_hbm, square_hbm, kernel_hbm, inverse_hbm,
+    image_hbm,
+    echo_ref, line_ref, table_ref, twiddle_ref, azimuth_ref, scale_ref, rate_ref, angle_ref, square_ref, kernel_ref, inverse_ref,
     image_ref,
-    echo_ref, line_ref, table_ref, twiddle_ref, azimuth_ref, scale_ref, rate_ref, angle_ref, square_ref, kernel_ref,
     chirp_ref, curve_ref, taps_ref, bit_ref, weight_ref, phase_ref,
     send_ref, got_ref, wide_ref, turned_ref, re_ref, im_ref, padded_ref, head_ref, tail_ref,
-    load_sems, y_sem, z_sem, send_sem, recv_sem, own_sem, halo_send, halo_recv,
+    load_sems, y_sem, z_sem, send_sem, recv_sem, own_sem, halo_send, halo_recv, image_sems,
 ):
     x, y, z, core = place()
     wide, narrow = device_at(x, y, z, core)
@@ -252,12 +250,14 @@
     for i, (source, target) in enumerate(
         (
             (chirp_hbm, line_ref), (table_hbm, table_ref), (twiddle_hbm, twiddle_ref),
-            (azimuth_hbm, azimuth_ref), (angle_hbm, angle_ref), (square_hbm, square_ref), (kernel_hbm, kernel_ref),
+            (angle_hbm, angle_ref), (square_hbm, square_ref), (kernel_hbm, kernel_ref),
             (scale_hbm.at[own_rows], scale_ref), (rate_hbm.at[own_rows], rate_ref),
+            (azimuth_hbm, azimuth_ref), (inverse_hbm, inverse_ref),
         )
     ):
         load = pltpu.make_async_copy(source, target, load_sems.at[pieces + i])
-        load.start()
+        if i < 8:
+            load.start()
         loads.append(load)
 
     barrier = pltpu.get_barrier_semaphore()
@@ -280,6 +280,8 @@
         lax.fori_loop(i * (EDGE // pieces), (i + 1) * (EDGE // pieces), spread, 0, unroll=8)
     for load in loads[:3]:
         load.wait()
+    for load in loads[8:]:
+        load.start()
 
     def lay(j, carry):
         for part in range(2):
@@ -340,15 +342,20 @@
     lax.fori_loop(ROWS // 4, ROWS // 2, pair, 0, unroll=UNROLL)
     low_half = lax.broadcasted_iota(jnp.int32, (ROWS, EDGE), 1) < EDGE // 2
 
-    def pack(u, carry):
+    def target(t):
+        z_step = jnp.where(core == 0, t % 8, (8 - t % 8) % 8)
+        x_step = (t // 8 + z_step) % 4
+        y_step = (t // 32 + z_step // 2) % 4
+        return device_at((x + x_step) % 4, (y + y_step) % 4, (z + z_step) % 8, 0)
+
+    def pack(t, carry):
+        to_wide, to_narrow = target(t)
+        u = to_wide * 2 + to_narrow // 2
         rows = pl.ds(pl.multiple_of(u * ROWS, ROWS), ROWS)
         re, im = turned_ref[0, rows, :], turned_ref[1, rows, :]
         send_ref[2 * u] = jnp.where(low_half, re, pltpu.roll(im, EDGE // 2, 1)).astype(BF16)
         send_ref[2 * u + 1] = jnp.where(low_half, pltpu.roll(re, EDGE // 2, 1), im).astype(BF16)
         return carry
-
-    lax.fori_loop(0, EDGE, pack, 0, unroll=8)
-    pl.semaphore_wait(z_sem, 7)
 
     def start(to_wide, to_narrow, to):
         pltpu.make_async_remote_copy(
@@ -357,17 +364,28 @@
         ).start()
 
     def spread_out(t, carry):
-        z_step = jnp.where(core == 0, t % 8, (8 - t % 8) % 8)
-        x_step = (t // 8 + z_step) % 4
-        y_step = (t // 32 + z_step // 2) % 4
-        to_wide, to_narrow = device_at((x + x_step) % 4, (y + y_step) % 4, (z + z_step) % 8, 0)
+        to_wide, to_narrow = target(t)
         to = to_wide * 4 + to_narrow
         start(to_wide, to_narrow, to)
         start(to_wide, to_narrow + 1, to + 1)
         return carry
 
+    lax.fori_loop(0, 16, pack, 0, unroll=8)
+    pl.semaphore_wait(z_sem, 7)
     start(wide, narrow + 1 - 2 * core, me + 1 - 2 * core)
-    lax.fori_loop(1, EDGE, spread_out, 0)
+    lax.fori_loop(1, 16, spread_out, 0)
+
+    def chunk(i, carry):
+        def packs(j, inner_carry):
+            for n in range(8):
+                pack(16 * i + 8 * j + n, 0)
+            return inner_carry
+
+        lax.fori_loop(0, 2, packs, 0)
+        lax.fori_loop(16 * i, 16 * i + 16, spread_out, 0)
+        return carry
+
+    lax.fori_loop(1, EDGE // 16, chunk, 0)
     own = pltpu.make_async_copy(send_ref.at[me], got_ref.at[me], own_sem)
     own.start()
     own.wait()
@@ -406,7 +424,7 @@
             [re, pltpu.roll(re, half, 1), im, pltpu.roll(im, half, 1)], axis=0
         ).astype(BF16)
         result = lax.dot_general(
-            left, block_table(azimuth_ref, k), (((0,), (0,)), ((), ())), preferred_element_type=F32
+            left, azimuth_ref[k], (((0,), (0,)), ((), ())), preferred_element_type=F32
         )
         for part in range(2):
             wide_ref[part, pl.ds(k, OWN, stride=LOW), :] = result[:OWN, part * EDGE : (part + 1) * EDGE]
@@ -441,53 +459,84 @@
         turned_ref[0, rows, :] = re
         turned_ref[1, rows, :] = im
 
-    def migrate(r):
+    def migrate(r, halves):
         migrate_rows(
-            r, scale_ref[scale_row, scale_column + r], padded_ref, bit_ref, weight_ref, phase_ref, store
+            r, scale_ref[scale_row, scale_column + r], halves, padded_ref, bit_ref, weight_ref, phase_ref, store
         )
 
     def inner(r, carry):
-        migrate(r)
+        migrate(r, (0, 1))
         return carry
 
     lax.fori_loop(HALO, OWN - HALO, inner, 0)
-    for halo in halos:
-        halo.wait()
-
-    def edge(r, carry):
-        for part in range(2):
-            padded_ref[part, r] = jnp.where(me == 0, jnp.zeros((LOW, EDGE), BF16), head_ref[part, r])
-            padded_ref[part, HALO + OWN + r] = jnp.where(
-                me == DEVICES - 1, jnp.zeros((LOW, EDGE), BF16), tail_ref[part, r]
-            )
-        return carry
-
-    lax.fori_loop(0, HALO, edge, 0)
-
-    def outer(i, carry):
-        migrate(jnp.where(i < HALO, i, i + OWN - 2 * HALO))
-        return carry
-
-    lax.fori_loop(0, 2 * HALO, outer, 0)
-
-    def back(k, carry):
-        left = jnp.concatenate(
-            [turned_ref[part, pl.ds(k, OWN, stride=LOW), :] for part in range(2)], axis=1
-        ).astype(BF16)
-        result = lax.dot_general(
-            left, block_table(azimuth_ref, k), (((1,), (1,)), ((), ())), preferred_element_type=F32
-        )
-        re_ref[k] = result[:, :EDGE]
-        im_ref[k] = result[:, EDGE:]
-        return carry
-
-    lax.fori_loop(0, LOW, back, 0, unroll=4)
 
     def finish(h, rows, re, im):
         image_ref[0, rows, h * EDGE : (h + 1) * EDGE] = re.astype(BF16)
         image_ref[1, rows, h * EDGE : (h + 1) * EDGE] = im.astype(BF16)
 
-    low_transform(re_ref, im_ref, 1, 16, finish)
+    def invert(spans, first, stride, begin=None):
+        def back(k, carry):
+            left = jnp.concatenate(
+                [
+                    jnp.concatenate(
+                        [turned_ref[part, pl.ds(start * LOW + k, count, stride=LOW), :] for start, count in spans], axis=0
+                    )
+                    for part in range(2)
+                ],
+                axis=1,
+            ).astype(BF16)
+            result = dot(left, inverse_ref[k])
+            done = 0
+            for start, count in spans:
+                re_ref[k, start : start + count, :] = result[done : done + count, :EDGE]
+                im_ref[k, start : start + count, :] = result[done : done + count, EDGE:]
+                done += count
+            return carry
+
+        if begin is not None:
+            lax.fori_loop(begin, begin + LOW // 2, back, 0, unroll=4)
+        else:
+            lax.fori_loop(0, LOW, back, 0, unroll=4)
+        if begin == 0:
+            return []
+        low_transform(re_ref, im_ref, 1, 16, finish, first, 2, stride)
+        copies = []
+        for start, count in spans:
+            rows = pl.ds(start, count)
+            copies.append(
+                pltpu.make_async_copy(
+                    image_ref.at[:, rows, :], image_hbm.at[:, rows, :], image_sems.at[start // HALO]
+                )
+            )
+            copies[-1].start()
+        return copies
+
+    writes = invert([(HALO, 2 * HALO)], HALO, HALO)
+    for h in range(2):
+        for halo in halos[2 * h : 2 * h + 2]:
+            halo.wait()
+
+        def edge(r, carry, h=h):
+            k_rows = pl.ds(16 * h, 16)
+            empty = jnp.zeros((16, EDGE), BF16)
+            for part in range(2):
+                padded_ref[part, r, k_rows, :] = jnp.where(me == 0, empty, head_ref[part, r, k_rows, :])
+                padded_ref[part, HALO + OWN + r, k_rows, :] = jnp.where(
+                    me == DEVICES - 1, empty, tail_ref[part, r, k_rows, :]
+                )
+            return carry
+
+        lax.fori_loop(0, HALO, edge, 0, unroll=4)
+
+        def outer(i, carry, h=h):
+            for n in range(2):
+                migrate(i + n * 3 * HALO, (h,))
+            return carry
+
+        lax.fori_loop(0, HALO, outer, 0)
+        writes += invert([(0, HALO), (3 * HALO, HALO)], 0, 3 * HALO, 16 * h)
+    for write in writes:
+        write.wait()
 
 
 UNROLL = 2
@@ -500,6 +549,7 @@
     scratch += [pltpu.SMEM((8, EDGE), jnp.int32), pltpu.SMEM((8, EDGE), F32)]
     scratch += [pltpu.VMEM(operand.shape, operand.dtype) for operand in operands[7:]]
     scratch += [
+        pltpu.VMEM((2, OWN, PULSES), BF16),
         pltpu.VMEM((2, EDGE, EDGE), F32),
         pltpu.VMEM((LOW, EDGE), F32),
         pltpu.VMEM((PHASES * TAPS, 16, EDGE), BF16),
@@ -515,7 +565,7 @@
         pltpu.VMEM((2, 2 * HALO + OWN + 8, LOW, EDGE), BF16),
         pltpu.VMEM((2, HALO, LOW, EDGE), BF16),
         pltpu.VMEM((2, HALO, LOW, EDGE), BF16),
-        pltpu.SemaphoreType.DMA((13,)),
+        pltpu.SemaphoreType.DMA((14,)),
         pltpu.SemaphoreType.REGULAR,
         pltpu.SemaphoreType.REGULAR,
         pltpu.SemaphoreType.DMA,
@@ -523,12 +573,13 @@
         pltpu.SemaphoreType.DMA,
         pltpu.SemaphoreType.DMA((4,)),
         pltpu.SemaphoreType.DMA((4,)),
+        pltpu.SemaphoreType.DMA((4,)),
     ]
     return pl.pallas_call(
         main_kernel,
         out_shape=jax.ShapeDtypeStruct((2, OWN, PULSES), BF16),
-        in_specs=[pl.BlockSpec(memory_space=pl.ANY)] * 10,
-        out_specs=pl.BlockSpec(memory_space=pltpu.VMEM),
+        in_specs=[pl.BlockSpec(memory_space=pl.ANY)] * 11,
+        out_specs=pl.BlockSpec(memory_space=pl.ANY),
         scratch_shapes=scratch,
         compiler_params=pltpu.CompilerParams(
             collective_id=0, has_side_effects=True, vmem_limit_bytes=VMEM_BYTES
@@ -539,13 +590,14 @@
 
 def shards(echoes, chirp_spectrum, fm_rate, range_scale, doppler_curve, kernels):
     tables, twiddles = range_tables()
+    forward, inverse = azimuth_tables()
     index = np.arange(PULSES)
     signed = (index + PULSES // 2) % PULSES - PULSES // 2
     square = np.ascontiguousarray((signed * signed).astype(np.float32).reshape(EDGE, LOW).T)
     return focused_image(
-        echoes, chirp_spectrum, jnp.asarray(tables), jnp.asarray(twiddles), jnp.asarray(azimuth_tables()),
+        echoes, chirp_spectrum, jnp.asarray(tables), jnp.asarray(twiddles), jnp.asarray(forward),
         range_scale.reshape(EDGE, EDGE), fm_rate.reshape(EDGE, EDGE),
-        doppler_curve.reshape(LOW, EDGE), jnp.asarray(square), kernels,
+        doppler_curve.reshape(LOW, EDGE), jnp.asarray(square), kernels, jnp.asarray(inverse),
     )
 
 

time: 64.5 us -> 62.7 us (0.972)
  Pallas kernels: 62.1 us -> 60.2 us
    pallas_call x1, Pallas kernels: 62.1 us -> 60.2 us  [focused_image(): pl.pallas_call(main_kernel, out_shape=jax.ShapeDtypeStruct((2, OWN, PULSE...]
where the time goes in v4:
time: 62.7 us; the launch traced here: 62.5 us
  Pallas kernels  60.2 us (96%)
  local copies, waits for them, and re-layouts  2.29 us (4%)
    pallas_call x1, Pallas kernels, focused_image(): pl.pallas_call(main_kernel, out_shape=jax.ShapeDtypeStruct((2, OWN, PULSE...  60.2 us
    unnamed x1, local copies, waits for them, and re-layouts  2.29 us

profile of v4, /device:TPU:1, one launch (start us, length us, event | category | flops | bytes accessed | tf_op | source)
XLA Modules:
  0.0 62.5 jit_solution(14789892957751313305)
XLA Ops:
  0.0 60.2 %focused_image.1 = bf16[2,64,4096]{2,1,0:T(8,128)(2,1)} custom-call(bf16[2,16,16384]{2,1,0:T(8,128)(2,1)} %echo_hbm.1, f32[2,16384]{1,0:T(2,128)} %chirp_hbm.1, bf16[4,256,256]{2,1,0:T(8,128)(2,1)} %constant.10.clone.table_hbm, f32[2,128,128]{2,1,0:T(8,128)} %constant.11.clone.twiddle_hbm, bf16[32,256,256]{2,1,0:T(8,128)(2,1)} %constant.12.clone.azimuth_hbm, ...), custom_call_target="tpu_custom_call" | custom-call | tf_op jit(solution)/shard_map/focused_image/pallas_call | solution.py:578
  60.2 2.3 %copy.13 = bf16[2,64,4096]{2,1,0:T(8,128)(2,1)} copy(bf16[2,64,4096]{2,1,0:T(8,128)(2,1)} %focused_image.1) | data formatting | bytes 2097152

commit v5 on v4

--- a/solution.py
+++ b/solution.py
@@ -99,22 +99,6 @@
     pl.semaphore_signal(
         semaphore, inc=1, device_id={"wide": wide, "narrow": narrow}, device_id_type=MESH_IDS
     )
-
-
-def split_pairs(got_ref, re_ref, im_ref):
-    half = EDGE // 2
-    low_half = lax.broadcasted_iota(jnp.int32, (ROWS, EDGE), 1) < half
-
-    def step(m, carry):
-        for g in range(half // ROWS):
-            near = got_ref[m * 8 + g].astype(F32)
-            far = got_ref[m * 8 + 4 + g].astype(F32)
-            rows = pl.ds(g * ROWS, ROWS)
-            re_ref[m, rows, :] = jnp.where(low_half, near, pltpu.roll(far, half, 1))
-            im_ref[m, rows, :] = jnp.where(low_half, pltpu.roll(near, half, 1), far)
-        return carry
-
-    lax.fori_loop(0, LOW, step, 0, unroll=2)
 
 
 def low_transform(re_ref, im_ref, sign, block, store, first=0, count=8, stride=8):
@@ -357,22 +341,22 @@
         send_ref[2 * u + 1] = jnp.where(low_half, pltpu.roll(re, EDGE // 2, 1), im).astype(BF16)
         return carry
 
-    def start(to_wide, to_narrow, to):
+    def start(to_wide, to_narrow, to, group):
         pltpu.make_async_remote_copy(
-            send_ref.at[to], got_ref.at[me], send_sem, recv_sem,
+            send_ref.at[to], got_ref.at[me], send_sem, recv_sem.at[group],
             device_id={"wide": to_wide, "narrow": to_narrow}, device_id_type=MESH_IDS,
         ).start()
 
     def spread_out(t, carry):
         to_wide, to_narrow = target(t)
         to = to_wide * 4 + to_narrow
-        start(to_wide, to_narrow, to)
-        start(to_wide, to_narrow + 1, to + 1)
+        start(to_wide, to_narrow, to, t // 16)
+        start(to_wide, to_narrow + 1, to + 1, t // 16)
         return carry
 
     lax.fori_loop(0, 16, pack, 0, unroll=8)
     pl.semaphore_wait(z_sem, 7)
-    start(wide, narrow + 1 - 2 * core, me + 1 - 2 * core)
+    start(wide, narrow + 1 - 2 * core, me + 1 - 2 * core, 0)
     lax.fori_loop(1, 16, spread_out, 0)
 
     def chunk(i, carry):
@@ -406,16 +390,52 @@
         return carry
 
     lax.fori_loop(0, OWN, prepare, 0)
-    others = pltpu.make_async_remote_copy(
-        send_ref.at[pl.ds(0, DEVICES - 1)], got_ref.at[pl.ds(0, DEVICES - 1)], send_sem, recv_sem,
-        device_id={"wide": wide, "narrow": (narrow + 1) % 4}, device_id_type=MESH_IDS,
-    )
-    others.wait_send()
-    others.wait_recv()
-
-
     half = EDGE // 2
-    split_pairs(got_ref, re_ref, im_ref)
+    upper_half = lax.broadcasted_iota(jnp.int32, (ROWS, EDGE), 1) // half
+
+    def messages(first, count, semaphore):
+        return pltpu.make_async_remote_copy(
+            send_ref.at[pl.ds(first, count)], got_ref.at[pl.ds(first, count)], send_sem, semaphore,
+            device_id={"wide": wide, "narrow": (narrow + 1) % 4}, device_id_type=MESH_IDS,
+        )
+
+    def take(t, from_core):
+        z_step = t % 8 if from_core == 0 else (8 - t % 8) % 8
+        x_step = (t // 8 + z_step) % 4
+        y_step = (t // 32 + z_step // 2) % 4
+        from_x = (x - x_step + 4) % 4
+        from_wide, from_narrow = device_at(from_x, (y - y_step + 4) % 4, (z - z_step + 8) % 8, from_core)
+        odd = from_x % 2
+        message = got_ref[from_wide * 4 + from_narrow].astype(F32)
+        turned = pltpu.roll(message, half, 1)
+        m = from_wide // 2
+        rows = pl.ds(pl.multiple_of(from_narrow * ROWS, ROWS), ROWS)
+        kept = upper_half == odd
+        re_ref[m, rows, :] = jnp.where(kept, jnp.where(odd == 0, message, turned), re_ref[m, rows, :])
+        im_ref[m, rows, :] = jnp.where(kept, jnp.where(odd == 0, turned, message), im_ref[m, rows, :])
+
+    def takes(t, carry):
+        take(t, 0)
+        take(t, 1)
+        return carry
+
+    messages(0, 31, recv_sem.at[0]).wait_recv()
+    lax.fori_loop(0, 16, takes, 0, unroll=2)
+
+    def group(i, carry):
+        messages(0, 32, recv_sem.at[i]).wait_recv()
+
+        def two(j, inner_carry):
+            takes(16 * i + 2 * j, 0)
+            takes(16 * i + 2 * j + 1, 0)
+            return inner_carry
+
+        lax.fori_loop(0, 8, two, 0)
+        return carry
+
+    lax.fori_loop(1, 8, group, 0)
+    messages(0, DEVICES - 1, recv_sem.at[0]).wait_send()
+
     low_transform(re_ref, im_ref, -1, 8, low_store(re_ref, im_ref))
 
     def high(k, carry):
@@ -569,7 +589,7 @@
         pltpu.SemaphoreType.REGULAR,
         pltpu.SemaphoreType.REGULAR,
         pltpu.SemaphoreType.DMA,
-        pltpu.SemaphoreType.DMA,
+        pltpu.SemaphoreType.DMA((8,)),
         pltpu.SemaphoreType.DMA,
         pltpu.SemaphoreType.DMA((4,)),
         pltpu.SemaphoreType.DMA((4,)),

time: 62.7 us -> 63.2 us (level)
  no operation moved by 1% of the time
where the time goes in v5:
time: 63.2 us; the launch traced here: 63 us
  Pallas kernels  60.7 us (96%)
  local copies, waits for them, and re-layouts  2.29 us (4%)
    pallas_call x1, Pallas kernels, focused_image(): pl.pallas_call(main_kernel, out_shape=jax.ShapeDtypeStruct((2, OWN, PULSE...  60.7 us
    unnamed x1, local copies, waits for them, and re-layouts  2.29 us

profile of v5, /device:TPU:1, one launch (start us, length us, event | category | flops | bytes accessed | tf_op | source)
XLA Modules:
  0.0 63.0 jit_solution(13552249183987408575)
XLA Ops:
  0.0 60.7 %focused_image.1 = bf16[2,64,4096]{2,1,0:T(8,128)(2,1)} custom-call(bf16[2,16,16384]{2,1,0:T(8,128)(2,1)} %echo_hbm.1, f32[2,16384]{1,0:T(2,128)} %chirp_hbm.1, bf16[4,256,256]{2,1,0:T(8,128)(2,1)} %constant.10.clone.table_hbm, f32[2,128,128]{2,1,0:T(8,128)} %constant.11.clone.twiddle_hbm, bf16[32,256,256]{2,1,0:T(8,128)(2,1)} %constant.12.clone.azimuth_hbm, ...), custom_call_target="tpu_custom_call" | custom-call | tf_op jit(solution)/shard_map/focused_image/pallas_call | solution.py:598
  60.7 2.3 %copy.13 = bf16[2,64,4096]{2,1,0:T(8,128)(2,1)} copy(bf16[2,64,4096]{2,1,0:T(8,128)(2,1)} %focused_image.1) | data formatting | bytes 2097152
